TPU v7x, 32 devices: a whole 2x2x4 slice. The times are simulated.
32 devices in a mesh: crops: 16 (over z, y, x), rows: 2 (over core).
Axes of the slice: x: 2, y: 2, z: 4, core: 2. Of those that a mesh axis runs over, the one named last changes fastest.
Arguments:
- image_big: bfloat16 [192, 14, 14, 1024], P('crops', 'rows'), may hold values from -6 to 6
- image_small: bfloat16 [128, 10, 10, 1024], P('crops', 'rows'), may hold values from -6 to 6
- view_big: int32 [192], P('crops'), may hold values from 0 to 1, as said below
- view_small: int32 [128], P('crops'), may hold values from 0 to 1
- inner_first: bfloat16 [1024, 256], replicated, may hold values from -0.1875 to 0.1875
- spatial_first: bfloat16 [3, 3, 256, 256], replicated, may hold values from -0.125 to 0.125
- outer_first: bfloat16 [256, 1024], replicated, may hold values from -0.375 to 0.375
- norms_first: float32 [2, 1536], replicated, may hold values from 0.25 to 1.75
- inner_second: bfloat16 [1024, 512], replicated, may hold values from -0.1875 to 0.1875
- spatial_second: bfloat16 [3, 3, 512, 512], replicated, may hold values from -0.09375 to 0.09375
- outer_second: bfloat16 [512, 2048], replicated, may hold values from -0.25 to 0.25
- skip_second: bfloat16 [1024, 2048], replicated, may hold values from -0.1875 to 0.1875
- norms_second: float32 [2, 5120], replicated, may hold values from 0.25 to 1.75
- cotangent_big: bfloat16 [192, 7, 7, 2048], P(('crops', 'rows')), may hold values from -6 to 6
- cotangent_small: bfloat16 [128, 5, 5, 2048], P(('crops', 'rows')), may hold values from -6 to 6
Outputs:
- result_big: bfloat16 [192, 7, 7, 2048], P(('crops', 'rows'))
- result_small: bfloat16 [128, 5, 5, 2048], P(('crops', 'rows'))
- gradient_big: bfloat16 [192, 14, 14, 1024], P('crops', 'rows')
- gradient_small: bfloat16 [128, 10, 10, 1024], P('crops', 'rows')
- inner_first_grad: float32 [1024, 256], replicated
- spatial_first_grad: float32 [3, 3, 256, 256], replicated
- outer_first_grad: float32 [256, 1024], replicated
- norms_first_grad: float32 [2, 1536], replicated
- inner_second_grad: float32 [1024, 512], replicated
- spatial_second_grad: float32 [3, 3, 512, 512], replicated
- outer_second_grad: float32 [512, 2048], replicated
- skip_second_grad: float32 [1024, 2048], replicated
- norms_second_grad: float32 [2, 5120], replicated
Inputs may be any that keep to these rules, and one draw needn't show every extreme that they name: `view_big`: the first larger crop is of view 0 and the second of view 1.
All inputs are finite; a program needn't handle non-finite values.
Results may differ from a plain program's by a relative error of at most 0.017.
Values may be sent and summed in bfloat16 or wider, within the bound.
A program may use at most 256 MiB of HBM per device.

v0:
```python
import functools

import jax
import jax.numpy as jnp
from jax import lax
from jax.experimental import pallas as pl
from jax.experimental.pallas import tpu as pltpu
from jax.sharding import PartitionSpec as P

HIGH = lax.Precision.HIGHEST
EPS = 1e-05
MESH = pl.DeviceIdType.MESH
F32 = jnp.float32
BF16 = jnp.bfloat16


class Maps:
    def __init__(self, count, edge, row0, crop0, guard0, out0):
        self.count, self.edge = count, edge
        self.row0, self.crop0, self.guard0, self.out0 = row0, crop0, guard0, out0
        self.rows = edge * 16
        self.guard = (edge + 1) * 16
        self.half = edge // 2
        self.out = self.half * 8
        self.pixels = edge * edge


def geometry(nb, eb, ns, es):
    big = Maps(nb, eb, 0, 0, 16, 0)
    small = Maps(ns, es, nb * big.rows, nb, 16 + nb * big.guard, nb * big.out)
    total = small.row0 + ns * small.rows
    guarded = small.guard0 + ns * small.guard
    out = small.out0 + ns * small.out
    return (big, small), total, guarded, out


def al(x, m=16):
    return x if isinstance(x, int) else pl.multiple_of(x, m)


def span(start, size, m=16):
    return pl.ds(al(start, m), size)


def repeat(count, body):
    def step(i, carry):
        body(i)
        return carry

    lax.fori_loop(0, count, step, 0)


def mm(a, b):
    return jnp.dot(a, b, preferred_element_type=F32)


def mm_nt(a, b):
    return lax.dot_general(a, b, (((1,), (1,)), ((), ())), preferred_element_type=F32)


def mm_tn(a, b):
    return lax.dot_general(a, b, (((0,), (0,)), ((), ())), preferred_element_type=F32)


CA = 0.7978845608028654
CB = 0.7978845608028654 * 0.044715


def act(u):
    t = jnp.tanh(u * (CA + CB * (u * u)))
    return 0.5 * u * (1.0 + t)


def act_slope(u):
    s = u * u
    t = jnp.tanh(u * (CA + CB * s))
    rise = (0.5 * u) * (CA + (3.0 * CB) * s)
    return 0.5 * (1.0 + t) + (1.0 - t * t) * rise


def act_both(u):
    s = u * u
    t = jnp.tanh(u * (CA + CB * s))
    hu = 0.5 * u
    lift = 0.5 * (1.0 + t)
    slope = lift + (1.0 - t * t) * (hu * (CA + (3.0 * CB) * s))
    return u * lift, slope


def keep(width, pitch, edge):
    return lax.broadcasted_iota(jnp.int32, (pitch, width), 0) < edge


def masked(x, mask):
    rows = x.reshape(x.shape[0] // mask.shape[0], mask.shape[0], x.shape[1])
    return jnp.where(mask[None], rows, 0.0).reshape(x.shape)


def tile_sum(x):
    return jnp.sum(x.reshape(x.shape[0] // 8, 8, x.shape[1]), axis=0)


def pieces(width):
    return (4, width // 4) if width >= 512 else (width // 128, 128)


class Links:
    def __init__(self, crops, near, far, near_s, near_r, far_s, far_r):
        self.group = 4 if crops % 4 == 0 else 1
        self.outers = crops // self.group
        self.k, self.r = lax.axis_index("crops"), lax.axis_index("rows")
        inner, self.outer = lax.rem(self.k, self.group), self.k // self.group
        self.wide = 2 * self.group
        self.me = inner * 2 + self.r
        self.peers, self.others = [], []
        for d in range(1, self.wide):
            p = lax.rem(self.me + d, self.wide)
            self.peers.append((self.outer * self.group + p // 2, lax.rem(p, 2)))
        for d in range(1, self.outers):
            self.others.append((lax.rem(self.outer + d, self.outers) * self.group + inner, self.r))
        self.near, self.far = near, far
        self.sems = (near_s, near_r, far_s, far_r)
        self.live = {}

    def greet(self, extra=()):
        barrier = pltpu.get_barrier_semaphore()
        peers = self.peers + self.others + list(extra)
        for peer in peers:
            pl.semaphore_signal(barrier, inc=1, device_id=peer, device_id_type=MESH)
        pl.semaphore_wait(barrier, len(peers))

    def send_near(self, e, block):
        self.near[e][self.me] = block[...]
        self.live[e, 0] = []
        for d, peer in enumerate(self.peers):
            copy = pltpu.make_async_remote_copy(
                src_ref=block,
                dst_ref=self.near[e].at[self.me],
                send_sem=self.sems[0].at[e, d],
                recv_sem=self.sems[1].at[e, d],
                device_id=peer,
                device_id_type=MESH,
            )
            copy.start()
            self.live[e, 0].append(copy)

    def wait_near(self, e):
        for copy in self.live[e, 0]:
            copy.wait_recv()

    def send_far(self, e):
        self.live[e, 1] = []
        place = self.far[e].at[self.outer]
        for d, peer in enumerate(self.others):
            copy = pltpu.make_async_remote_copy(
                src_ref=place,
                dst_ref=place,
                send_sem=self.sems[2].at[e, d],
                recv_sem=self.sems[3].at[e, d],
                device_id=peer,
                device_id_type=MESH,
            )
            copy.start()
            self.live[e, 1].append(copy)

    def wait_far(self, e):
        for copy in self.live[e, 1]:
            copy.wait_recv()

    def finish(self):
        for copies in self.live.values():
            for copy in copies:
                copy.wait_send()


def fold_moments(buf, tallies, count, scale):
    sums, total = buf[0, 0:8, :], tallies[0]
    for i in range(1, count):
        sums = sums + buf[i, 0:8, :]
        total = total + tallies[i]
    mean = sums * (1.0 / jnp.maximum(total * scale, 1.0))
    spread = None
    for i in range(count):
        n = tallies[i] * scale
        apart = buf[i, 0:8, :] * (1.0 / jnp.maximum(n, 1.0)) - mean
        term = buf[i, 8:16, :] + n * apart * apart
        spread = term if spread is None else spread + term
    return sums, spread, total


def fold_sums(buf, count):
    total = buf[0]
    for i in range(1, count):
        total = total + buf[i]
    return total


def exchange_shapes(widths, tiles, crops):
    group = 4 if crops % 4 == 0 else 1
    outers = crops // group
    blocks, near, far = [], [], []
    for width, tile in zip(widths, tiles):
        lanes = pieces(width)[1]
        blocks.append(pltpu.VMEM((8 * tile, lanes), F32))
        near.append(pltpu.VMEM((2 * group, 8 * tile, lanes), F32))
        far.append(pltpu.VMEM((outers, 8 * tile, lanes), F32))
    e = len(widths)
    sems = [
        pltpu.SemaphoreType.DMA((e, 2 * group - 1)),
        pltpu.SemaphoreType.DMA((e, 2 * group - 1)),
        pltpu.SemaphoreType.DMA((e, max(outers - 1, 1))),
        pltpu.SemaphoreType.DMA((e, max(outers - 1, 1))),
    ]
    return blocks + near + far + sems


def take(refs, count):
    return list(refs[:count]), refs[count:]


def pack(block, tile, rows, width):
    count, lanes = pieces(width)
    for q in range(count):
        for v in range(2):
            block[tile * 8 + 2 * q + v : tile * 8 + 2 * q + v + 1, :] = rows[v][:, q * lanes : (q + 1) * lanes]


def unpack(table, row, tile, width):
    count, lanes = pieces(width)
    for q in range(count):
        table[row : row + 2, q * lanes : (q + 1) * lanes] = tile[2 * q : 2 * q + 2, :]


def crop_stats(ref, row0, rows, step, width, edge, pitch, pixels, crop, cs, cm, col0=0):
    mask = keep(width, pitch, edge)
    zero = jnp.zeros((8, width), F32)
    cols = pl.ds(col0, width) if isinstance(col0, int) else pl.ds(pl.multiple_of(col0, 128), width)
    near = min(8, edge)
    first = masked(ref[span(row0, 8, 8), cols], keep(width, 8, edge))
    pivot = jnp.sum(first, axis=0, keepdims=True) * (1.0 / near)

    def tile(i, acc):
        d = masked(ref[span(row0 + i * step, step, 8), cols] - pivot, mask)
        return acc[0] + tile_sum(d), acc[1] + tile_sum(d * d)

    if rows == step:
        s, m = tile(0, (zero, zero))
    else:
        s, m = lax.fori_loop(0, rows // step, tile, (zero, zero))
    s = jnp.sum(s, axis=0, keepdims=True)
    m = jnp.sum(m, axis=0, keepdims=True)
    cs[pl.ds(crop, 1), cols] = s + pivot * float(pixels)
    cm[pl.ds(crop, 1), cols] = jnp.maximum(m - s * s * (1.0 / pixels), 0.0)


def local_moments(block, cs, cm, wcol, width, scale, tally=False):
    s, m = cs[:, 0:width], cm[:, 0:width]
    pix = wcol[:, 2:3] * scale
    mean_c = s * (1.0 / pix)
    sums, squares, tallies = [], [], []
    for v in range(2):
        w = wcol[:, v : v + 1]
        total = jnp.sum(w * s, axis=0, keepdims=True)
        n = jnp.sum(w * pix, axis=0, keepdims=True)
        apart = mean_c - total * (1.0 / jnp.maximum(n, 1.0))
        squares.append(jnp.sum(w * (m + pix * apart * apart), axis=0, keepdims=True))
        sums.append(total)
        tallies.append(n)
    pack(block, 0, sums, width)
    pack(block, 1, squares, width)
    if tally:
        lanes = pieces(width)[1]
        for q in range(4):
            for v in range(2):
                block[16 + 2 * q + v : 17 + 2 * q + v, :] = jnp.broadcast_to(tallies[v], (1, lanes))


def local_sums(block, parts, wcol, width):
    for tile, part in enumerate(parts):
        s = part[:, 0:width]
        pack(block, tile, [jnp.sum(wcol[:, v : v + 1] * s, axis=0, keepdims=True) for v in range(2)], width)


def view_tables(sets, core, views, wv, wcol):
    row = lax.broadcasted_iota(jnp.int32, wcol.shape, 0)
    lane = lax.broadcasted_iota(jnp.int32, wcol.shape, 1)
    table = jnp.where(lane == 2, 1.0, 0.0)
    for m, view in zip(sets, views):
        for c in range(m.count):
            second = view[core * m.count + c].astype(F32)
            pair = (1.0 - second, second, float(m.pixels))
            for v in range(3):
                table = jnp.where((row == m.crop0 + c) & (lane == v), pair[v], table)
            wv[0, m.crop0 + c] = pair[0]
            wv[1, m.crop0 + c] = pair[1]
    wcol[...] = table


def by_view(wv, crop, pair):
    return wv[0, crop] * pair[0:1, :] + wv[1, crop] * pair[1:2, :]


FWD_WIDTHS = (256, 256, 1024, 512, 2048, 512, 2048, 2048)


def forward_kernel(sets, total, guarded, outs, crops, dims, *refs):
    c3, cin, c4, cout = dims
    (
        vb, vs, norms1, norms2,
        img_b, img_s, cot_hbm, w1_h, wsp1_h, w3_h, w4_h, w5_h, w6_h, w7_h,
    ), refs = refs[:14], refs[14:]
    (
        o_img, o_z1, o_h1, o_z2, o_h2, o_blk, o_z4, o_x5, o_z5, o_h5, o_xe, o_res, o_d6, o_d7,
        o_st1, o_st2, o_st3, o_st4, o_st7, o_st5, o_st6, o_sq, o_tally,
    ), refs = refs[:23], refs[23:]
    (
        img, z1, h1, z2, h2, zt, blk, eb, z4, xe, z7, hp, x5, z5, h5, z6, cot,
        w1, wsp1, w3, w4, w5, w6, w7, cs, cm, ck,
        st1, st2, st3, st4, st7, st5, st6, sq, tally_v, wv, wcol,
    ), refs = refs[:38], refs[38:]
    e = len(FWD_WIDTHS)
    blocks, refs = take(refs, e)
    near, refs = take(refs, e)
    far, refs = take(refs, e)
    ns_, nr_, fs_, fr_ = refs[:4]
    load_sem, img_sem, img_send, img_recv, out_sem = refs[4:]
    links = Links(crops, near, far, ns_, nr_, fs_, fr_)
    k, core = links.k, links.r
    sibling = (k, 1 - core)
    f = F32

    loads = []
    for i, (src, dst) in enumerate(
        ((w1_h, w1), (wsp1_h, wsp1), (w3_h, w3), (w4_h, w4), (w5_h, w5), (w6_h, w6), (w7_h, w7), (cot_hbm, cot))
    ):
        loads.append(pltpu.make_async_copy(src, dst, load_sem.at[i]))
    own, swaps = [], []
    for at, (m, src) in enumerate(zip(sets, (img_b, img_s))):
        part = m.rows // 2
        for c in range(m.count):
            i = m.crop0 + c
            place = img.at[span(m.row0 + c * m.rows + core * part, part)]
            own.append(
                pltpu.make_async_copy(
                    src.at[span((core * m.count + c) * part, part)], place, img_sem.at[i]
                )
            )
            swaps.append(
                pltpu.make_async_remote_copy(
                    src_ref=src.at[span(((1 - core) * m.count + c) * part, part)],
                    dst_ref=place,
                    send_sem=img_send.at[i],
                    recv_sem=img_recv.at[i],
                    device_id=sibling,
                    device_id_type=MESH,
                )
            )
    for copy in own:
        copy.start()
    loads[0].start()
    links.greet()
    for copy in swaps:
        copy.start()

    view_tables(sets, core, (vb, vs), wv, wcol)
    out_copies = []

    def put(src, dst):
        copy = pltpu.make_async_copy(src, dst, out_sem.at[len(out_copies)])
        copy.start()
        out_copies.append(copy)

    for ref in (cs, cm, ck):
        ref[...] = jnp.zeros(ref.shape, f)
    for block in blocks:
        block[...] = jnp.zeros(block.shape, f)
    h1[0:16, :] = jnp.zeros((16, 3 * c3), BF16)
    for m in sets:
        for c in range(m.count):
            at = m.guard0 + c * m.guard + m.rows
            h1[at : at + 16, :] = jnp.zeros((16, 3 * c3), BF16)

    def near_tallies():
        return [near[0][i, 16:24, 0:1] for i in range(links.wide)]

    def far_tallies():
        return [far[0][i, 16:24, 0:1] for i in range(links.outers)]

    def meet_near(i, scale):
        links.wait_near(i)
        sums, spread, n = fold_moments(near[i], near_tallies(), links.wide, scale)
        place = far[i].at[links.outer]
        place[0:8, :] = sums
        place[8:16, :] = spread
        if i == 0:
            place[16:24, :] = jnp.broadcast_to(n, (8, near[0].shape[2]))
        links.send_far(i)

    def meet_far(i, scale, table, width):
        links.wait_far(i)
        sums, spread, n = fold_moments(far[i], far_tallies(), links.outers, scale)
        over = 1.0 / (n * scale)
        mean = sums * over
        inverse = lax.rsqrt(spread * over + EPS)
        unpack(table, 0, mean, width)
        unpack(table, 2, inverse, width)
        if i == 0:
            tally_v[...] = jnp.broadcast_to(n, (8, 128))

    loads[0].wait()
    for m in sets:

        def pair(p, m=m):
            r = m.row0 + p * 2 * m.rows
            for j in range(2):
                own[m.crop0 + 2 * p + j].wait()
                swaps[m.crop0 + 2 * p + j].wait_recv()
            z1[span(r, 2 * m.rows), :] = mm(img[span(r, 2 * m.rows), :], w1[...])
            for j in range(2):
                crop_stats(z1, r + j * m.rows, m.rows, m.rows // 2, c3, m.edge, 16, m.pixels, m.crop0 + 2 * p + j, cs, cm)

        for p in range(m.count // 2):
            pair(p)
            if m is sets[0] and p == 0:
                for copy in loads[1:]:
                    copy.start()
    local_moments(blocks[0], cs, cm, wcol, c3, 1.0, True)
    links.send_near(0, blocks[0])
    put(img, o_img)
    put(z1, o_z1)
    loads[1].wait()
    meet_near(0, 1.0)
    meet_far(0, 1.0, st1, c3)

    for m in sets:

        def pair(p, m=m):
            r = m.row0 + p * 2 * m.rows
            g = m.guard0 + p * 2 * m.guard
            for j in range(2):
                crop = m.crop0 + 2 * p + j
                mean = by_view(wv, crop, st1[0:2, :])
                scale = by_view(wv, crop, st1[2:4, :]) * norms1[0:1, 0:c3]
                shift = norms1[1:2, 0:c3] - mean * scale
                step = m.rows // 2
                mask = keep(c3, 16, m.edge)

                def tile(i):
                    z = z1[span(r + j * m.rows + i * step, step), :]
                    h = masked(act(z * scale + shift), mask)
                    rows = span(g + j * m.guard + i * step, step)
                    h1[rows, 0:c3] = pltpu.roll(h, 1, 0).astype(BF16)
                    h1[rows, c3 : 2 * c3] = h.astype(BF16)
                    h1[rows, 2 * c3 : 3 * c3] = pltpu.roll(h, step - 1, 0).astype(BF16)

                repeat(2, tile)
            size = 2 * m.rows + 16
            z = mm(h1[span(g - 16, size), :], wsp1[0]) + mm(h1[span(g, size), :], wsp1[1])
            z = z + mm(h1[span(g + 16, size), :], wsp1[2])
            z2[span(r, m.rows), :] = z[0 : m.rows]
            z2[span(r + m.rows, m.rows), :] = z[m.guard : m.guard + m.rows]
            for j in range(2):
                crop_stats(z2, r + j * m.rows, m.rows, m.rows // 2, c3, m.edge, 16, m.pixels, m.crop0 + 2 * p + j, cs, cm)

        repeat(m.count // 2, pair)
    local_moments(blocks[1], cs, cm, wcol, c3, 1.0)
    links.send_near(1, blocks[1])
    put(h1, o_h1)
    put(z2, o_z2)
    loads[2].wait()
    meet_near(1, 1.0)
    meet_far(1, 1.0, st2, c3)

    for m in sets:

        def pair(p, m=m):
            r = m.row0 + p * 2 * m.rows
            for j in range(2):
                crop = m.crop0 + 2 * p + j
                mean = by_view(wv, crop, st2[0:2, :])
                scale = by_view(wv, crop, st2[2:4, :]) * norms1[0:1, c3 : 2 * c3]
                shift = norms1[1:2, c3 : 2 * c3] - mean * scale
                step = m.rows // 2

                def tile(i):
                    rows = span(r + j * m.rows + i * step, step)
                    h2[rows, :] = act(z2[rows, :] * scale + shift).astype(BF16)

                repeat(2, tile)
            zt[0 : 2 * m.rows, :] = mm(h2[span(r, 2 * m.rows), :], w3[...])
            for j in range(2):
                crop_stats(zt, j * m.rows, m.rows, 32, cin, m.edge, 16, m.pixels, m.crop0 + 2 * p + j, cs, cm)

        repeat(m.count // 2, pair)
    local_moments(blocks[2], cs, cm, wcol, cin, 1.0)
    links.send_near(2, blocks[2])
    put(h2, o_h2)
    loads[3].wait()
    meet_near(2, 1.0)
    meet_far(2, 1.0, st3, cin)

    for m in sets:

        def pair(p, m=m):
            r = m.row0 + p * 2 * m.rows
            zt[0 : 2 * m.rows, :] = mm(h2[span(r, 2 * m.rows), :], w3[...])
            for j in range(2):
                crop = m.crop0 + 2 * p + j
                mean = by_view(wv, crop, st3[0:2, :])
                scale = by_view(wv, crop, st3[2:4, :]) * norms1[0:1, 2 * c3 :]
                shift = norms1[1:2, 2 * c3 :] - mean * scale

                def tile(i):
                    here = span(j * m.rows + i * 32, 32)
                    rows = span(r + j * m.rows + i * 32, 32)
                    u = zt[here, :] * scale + shift + img[rows, :].astype(f)
                    b = act(u)
                    blk[rows, :] = b.astype(BF16)
                    for q in range(cin // 128):
                        eb[q, span(j * m.rows // 2 + i * 16, 16), :] = b[0:16, q * 128 : (q + 1) * 128]

                repeat(m.rows // 32, tile)
            for q in range(cin // 128):
                picked = [eb[q, pl.ds(i * 16, 8, stride=2), :] for i in range(2 * m.half)]
                xe[span(m.out0 + p * 2 * m.out, 2 * m.out), q * 128 : (q + 1) * 128] = jnp.concatenate(
                    picked, axis=0
                ).astype(BF16)
            z4[span(r, 2 * m.rows), :] = mm(blk[span(r, 2 * m.rows), :], w4[...])
            for j in range(2):
                crop_stats(z4, r + j * m.rows, m.rows, 32, c4, m.edge, 16, m.pixels, m.crop0 + 2 * p + j, cs, cm)

        repeat(m.count // 2, pair)
    local_moments(blocks[3], cs, cm, wcol, c4, 1.0)
    links.send_near(3, blocks[3])
    put(blk, o_blk)
    put(z4, o_z4)
    put(xe, o_xe)
    loads[6].wait()

    def wide_product(a, w, z):
        def columns(n):
            cols = pl.ds(pl.multiple_of(n * 512, 512), 512)
            z[:, cols] = mm(a[...], w[:, cols])

        repeat(cout // 512, columns)

    def wide_stats(z):
        for m in sets:

            def crop_(c, m=m):
                def columns(n):
                    crop_stats(
                        z, m.out0 + c * m.out, m.out, m.out, 512, m.half, 8, m.half * m.half,
                        m.crop0 + c, cs, cm, n * 512,
                    )

                repeat(cout // 512, columns)

            repeat(m.count, crop_)

    wide_product(xe, w7, z7)
    meet_near(3, 1.0)
    wide_stats(z7)
    local_moments(blocks[4], cs, cm, wcol, cout, 0.25)
    links.send_near(4, blocks[4])
    meet_far(3, 1.0, st4, c4)

    loads[4].wait()
    lots = c4 // 128
    hp[:, 0:24, :] = jnp.zeros((lots, 24, 128), f)
    for m in sets:

        def pair(p, m=m):
            r = m.row0 + p * 2 * m.rows
            for j in range(2):
                crop = m.crop0 + 2 * p + j
                mean = by_view(wv, crop, st4[0:2, :])
                scale = by_view(wv, crop, st4[2:4, :]) * norms2[0:1, 0:c4]
                shift = norms2[1:2, 0:c4] - mean * scale
                mask = keep(c4, 16, m.edge)
                base = 24 + j * m.guard
                hp[:, base + m.rows : base + m.guard, :] = jnp.zeros((lots, 16, 128), f)

                def tile(i):
                    z = z4[span(r + j * m.rows + i * 32, 32), :]
                    h = masked(act(z * scale + shift), mask)
                    for q in range(lots):
                        hp[q, span(base + i * 32, 32, 8), :] = h[:, q * 128 : (q + 1) * 128]

                repeat(m.rows // 32, tile)
            for a in range(3):
                for b in range(3):
                    for q in range(lots):
                        picked = []
                        for j in range(2):
                            for i in range(m.half):
                                at = 24 + j * m.guard + (2 * i + a - 1) * 16 + b - 1
                                picked.append(hp[q, pl.ds(at, 8, stride=2), :])
                        tap = (3 * a + b) * c4 + q * 128
                        x5[span(m.out0 + p * 2 * m.out, 2 * m.out), tap : tap + 128] = jnp.concatenate(
                            picked, axis=0
                        ).astype(BF16)

        repeat(m.count // 2, pair)
    z5[...] = jnp.zeros(z5.shape, f)

    def taps(t):
        part = pl.ds(pl.multiple_of(t * 3 * c4, 128), 3 * c4)
        z5[...] += mm(x5[:, part], w5[part, :])

    repeat(3, taps)
    for m in sets:

        def crop_(c, m=m):
            crop_stats(z5, m.out0 + c * m.out, m.out, m.out, c4, m.half, 8, m.half * m.half, m.crop0 + c, cs, cm)

        repeat(m.count, crop_)
    local_moments(blocks[5], cs, cm, wcol, c4, 0.25)
    links.send_near(5, blocks[5])
    put(x5, o_x5)
    put(z5, o_z5)
    meet_near(4, 0.25)
    meet_near(5, 0.25)
    meet_far(4, 0.25, st7, cout)
    meet_far(5, 0.25, st5, c4)

    loads[5].wait()
    for m in sets:

        def pair(p, m=m):
            o = m.out0 + p * 2 * m.out
            halves = []
            for j in range(2):
                crop = m.crop0 + 2 * p + j
                mean = by_view(wv, crop, st5[0:2, :])
                scale = by_view(wv, crop, st5[2:4, :]) * norms2[0:1, c4 : 2 * c4]
                z = z5[span(o + j * m.out, m.out, 8), :]
                halves.append(act(z * scale + (norms2[1:2, c4 : 2 * c4] - mean * scale)))
            h5[span(o, 2 * m.out), :] = jnp.concatenate(halves, axis=0).astype(BF16)

        repeat(m.count // 2, pair)
    wide_product(h5, w6, z6)
    wide_stats(z6)
    local_moments(blocks[6], cs, cm, wcol, cout, 0.25)
    links.send_near(6, blocks[6])
    put(h5, o_h5)
    loads[7].wait()

    def center(ms):
        for m in ms:

            def crop_(c, m=m):
                def columns(n):
                    cols = pl.ds(pl.multiple_of(n * 512, 512), 512)
                    rows = span(m.out0 + c * m.out, m.out, 8)
                    mean = by_view(wv, m.crop0 + c, st7[0:2, cols])
                    z7[rows, cols] = (z7[rows, cols] - mean) * by_view(wv, m.crop0 + c, st7[2:4, cols])

                repeat(cout // 512, columns)

            repeat(m.count, crop_)

    center(sets[:1])
    meet_near(6, 0.25)
    center(sets[1:])
    meet_far(6, 0.25, st6, cout)

    out_copies[6].wait()
    g6, g7 = 2 * c4, 2 * c4 + cout
    lanes = 512
    for m in sets:

        def pair(p, m=m):
            o = m.out0 + p * 2 * m.out

            def columns(n):
                cols = pl.ds(pl.multiple_of(n * lanes, lanes), lanes)
                cols6 = pl.ds(pl.multiple_of(g6 + n * lanes, lanes), lanes)
                cols7 = pl.ds(pl.multiple_of(g7 + n * lanes, lanes), lanes)
                c = cot[span(o, 2 * m.out), cols].astype(f)
                mask = keep(lanes, 8, m.half)
                found = []
                for j in range(2):
                    crop = m.crop0 + 2 * p + j
                    rows = span(o + j * m.out, m.out, 8)
                    n6 = (z6[rows, cols] - by_view(wv, crop, st6[0:2, cols])) * by_view(wv, crop, st6[2:4, cols])
                    n7 = z7[rows, cols]
                    z6[rows, cols] = n6
                    u = n6 * norms2[0:1, cols6] + n7 * norms2[0:1, cols7] + (norms2[1:2, cols6] + norms2[1:2, cols7])
                    a, slope = act_both(u)
                    found.append(a)
                    up = masked(slope * c[j * m.out : (j + 1) * m.out], mask)
                    z4[span(n * outs + o + j * m.out, m.out, 8), :] = up
                    for to, part in ((cs, up), (cm, up * n6), (ck, up * n7)):
                        to[pl.ds(crop, 1), cols] = jnp.sum(tile_sum(part), axis=0, keepdims=True)
                w6[span(o, 2 * m.out), cols] = jnp.concatenate(found, axis=0).astype(BF16)

            repeat(cout // lanes, columns)

        repeat(m.count // 2, pair)
    local_sums(blocks[7], (cs, cm, ck), wcol, cout)
    links.send_near(7, blocks[7])
    put(w6.at[0:outs], o_res)
    links.wait_near(7)
    far[7][links.outer] = fold_sums(near[7], links.wide)
    links.send_far(7)
    links.wait_far(7)
    sums = fold_sums(far[7], links.outers)
    for t in range(3):
        unpack(sq, 2 * t, sums[8 * t : 8 * t + 8], cout)

    for m in sets:

        def pair(p, m=m):
            o = m.out0 + p * 2 * m.out

            def columns(n):
                cols = pl.ds(pl.multiple_of(n * lanes, lanes), lanes)
                mask = keep(lanes, 8, m.half)
                got6, got7 = [], []
                for j in range(2):
                    crop = m.crop0 + 2 * p + j
                    rows = span(o + j * m.out, m.out, 8)
                    up = z4[span(n * outs + o + j * m.out, m.out, 8), :]
                    over = wv[0, crop] * (4.0 / tally_v[0:1, 0:1]) + wv[1, crop] * (4.0 / tally_v[1:2, 0:1])
                    level = by_view(wv, crop, sq[0:2, cols]) * over
                    for got, z, st, at, t in ((got6, z6, st6, g6, 2), (got7, z7, st7, g7, 4)):
                        inv = by_view(wv, crop, st[2:4, cols])
                        gain = inv * norms2[0:1, pl.ds(pl.multiple_of(at + n * lanes, lanes), lanes)]
                        tilt = by_view(wv, crop, sq[t : t + 2, cols]) * over
                        got.append(masked(gain * (up - level - z[rows, cols] * tilt), mask))
                w7[span(o, 2 * m.out), cols] = jnp.concatenate(got6, axis=0).astype(BF16)
                w7[span(cin // 2 + o, 2 * m.out), cols] = jnp.concatenate(got7, axis=0).astype(BF16)

            repeat(cout // lanes, columns)

        repeat(m.count // 2, pair)
    put(w7.at[0:outs], o_d6)
    put(w7.at[cin // 2 : cin // 2 + outs], o_d7)
    for src, dst in (
        (st1, o_st1), (st2, o_st2), (st3, o_st3), (st4, o_st4), (st7, o_st7), (st5, o_st5), (st6, o_st6),
        (sq, o_sq), (tally_v, o_tally),
    ):
        put(src, dst)
    links.finish()
    for copy in swaps:
        copy.wait_send()
    for i, copy in enumerate(out_copies):
        if i != 6:
            copy.wait()


def flat_rows(tensor, pitch):
    n, h, w, c = tensor.shape
    return jnp.pad(tensor, ((0, 0), (0, 0), (0, pitch - w), (0, 0))).reshape(n * h * pitch, c)


def forward(images, cots, views, w, norms_first, norms_second, ident):
    crops = lax.axis_size("crops")
    nb, ns = images[0].shape[0] // 2, images[1].shape[0] // 2
    sets, total, guarded, outs = geometry(nb, images[0].shape[2], ns, images[1].shape[2])
    w1, wsp1, w3, w4, w5, w6, w7 = w
    cin, c3 = w1.shape
    c4, cout = w6.shape
    smem, vmem = pl.BlockSpec(memory_space=pltpu.SMEM), pl.BlockSpec(memory_space=pltpu.VMEM)
    hbm = pl.BlockSpec(memory_space=pl.ANY)
    shape = jax.ShapeDtypeStruct
    out_shape = [
        shape((total, cin), BF16), shape((total, c3), F32), shape((guarded, 3 * c3), BF16), shape((total, c3), F32),
        shape((total, c3), BF16), shape((total, cin), BF16), shape((total, c4), F32), shape((outs, 9 * c4), BF16),
        shape((outs, c4), F32), shape((outs, c4), BF16), shape((outs, cin), BF16), shape((outs, cout), BF16),
        shape((outs, cout), BF16), shape((outs, cout), BF16),
        shape((8, c3), F32), shape((8, c3), F32), shape((8, cin), F32), shape((8, c4), F32), shape((8, cout), F32),
        shape((8, c4), F32), shape((8, cout), F32), shape((8, cout), F32), shape((8, 128), F32),
    ]
    most = 2 * sets[0].rows
    scratch = [
        pltpu.VMEM((total, cin), BF16), pltpu.VMEM((total, c3), F32), pltpu.VMEM((guarded, 3 * c3), BF16),
        pltpu.VMEM((total, c3), F32), pltpu.VMEM((total, c3), BF16), pltpu.VMEM((most, cin), F32),
        pltpu.VMEM((total, cin), BF16), pltpu.VMEM((cin // 128, most // 2, 128), F32), pltpu.VMEM((total, c4), F32),
        pltpu.VMEM((outs, cin), BF16), pltpu.VMEM((outs, cout), F32), pltpu.VMEM((c4 // 128, 24 + 2 * sets[0].guard, 128), F32),
        pltpu.VMEM((outs, 9 * c4), BF16), pltpu.VMEM((outs, c4), F32),
        pltpu.VMEM((outs, c4), BF16), pltpu.VMEM((outs, cout), F32), pltpu.VMEM((outs, cout), BF16),
    ]
    scratch += [pltpu.VMEM(t.shape, BF16) for t in w]
    scratch += [pltpu.VMEM((16, cout), F32)] * 3
    scratch += [pltpu.VMEM((8, n), F32) for n in (c3, c3, cin, c4, cout, c4, cout, cout, 128)]
    scratch += [pltpu.SMEM((2, 16), F32), pltpu.VMEM((16, 128), F32)]
    scratch += exchange_shapes(FWD_WIDTHS, (3, 2, 2, 2, 2, 2, 2, 3), crops)
    scratch += [
        pltpu.SemaphoreType.DMA((8,)), pltpu.SemaphoreType.DMA((nb + ns,)), pltpu.SemaphoreType.DMA((nb + ns,)),
        pltpu.SemaphoreType.DMA((nb + ns,)), pltpu.SemaphoreType.DMA((23,)),
    ]
    got = pl.pallas_call(
        functools.partial(forward_kernel, sets, total, guarded, outs, crops, (c3, cin, c4, cout)),
        out_shape=out_shape,
        in_specs=[smem, smem, vmem, vmem] + [hbm] * 10,
        out_specs=[hbm] * len(out_shape),
        scratch_shapes=scratch,
        compiler_params=pltpu.CompilerParams(
            collective_id=ident, has_side_effects=True, vmem_limit_bytes=63 * 1024 * 1024
        ),
        name="forward",
    )(
        *views, norms_first, norms_second,
        flat_rows(images[0], 16), flat_rows(images[1], 16),
        jnp.concatenate([flat_rows(t, 8) for t in cots], axis=0), *w,
    )
    return sets, (total, guarded, outs), got


def share_plan(shapes, cuts):
    chunks = []
    for at, (height, width) in enumerate(shapes):
        down, across = cuts[at]
        half, high = width // 2 // across, height // down
        for c in range(down):
            for p in range(across):
                chunks.append((at, c * high, high, p * half, half))
    return chunks


class Share:
    def __init__(self, shapes, chunks, orders, bits, links, sources, outs, acc, recv0, recvs, sems, begin, leave):
        self.shapes, self.chunks, self.bits = shapes, chunks, bits
        self.k, self.core = links.k, links.r
        self.sources, self.outs, self.acc, self.recv0, self.recvs = sources, outs, acc, recv0, recvs
        self.send_sem, self.recv_sem, self.load_sem, self.store_sem = sems
        self.sibling = (self.k, 1 - self.core)
        self.total = 2 * bits + 2
        self.live, self.loads, self.stores, self.begin, self.leave, self.at = {}, {}, {}, begin, leave, 0
        digit = [lax.rem(self.k // (1 << b), 2) for b in range(bits)]
        self.stages, self.regions, self.kinds, self.slots = [], [], [], []
        for i, (at, row, height, col, width) in enumerate(chunks):
            stages = []
            for a, b in zip(*orders[i]):
                if a == b:
                    mine, step = digit[a], 1 << a
                else:
                    mine = digit[a] * (1 - self.core) + digit[b] * self.core
                    step = (1 << a) * (1 - self.core) + (1 << b) * self.core
                stages.append((mine, self.k + step * (1 - 2 * mine)))
            start, length, used = 0, height, 0
            region, kind, slot = [], [], []
            for s in range(bits):
                region.append((start, length))
                slot.append(used)
                if length % 32 == 0:
                    kind.append(True)
                    length //= 2
                    start = start + stages[s][0] * length
                else:
                    kind.append(False)
                used += length
            region.append((start, length))
            self.stages.append(stages)
            self.regions.append(region)
            self.kinds.append(kind)
            self.slots.append(slot)

    def send(self, i, t, src, dst, device):
        copy = pltpu.make_async_remote_copy(
            src_ref=src,
            dst_ref=dst,
            send_sem=self.send_sem.at[i, t],
            recv_sem=self.recv_sem.at[i, t],
            device_id=device,
            device_id_type=MESH,
        )
        copy.start()
        self.live[i, t] = copy

    def add(self, dst, at, src, src_at, length):
        block = 16
        while length % (block * 2) == 0 and block * 2 * dst.shape[1] <= 65536:
            block *= 2

        def step(j, carry):
            off = j * block
            rows = span(at + off, block)
            dst[rows, :] = dst[rows, :] + src[span(src_at + off, block), :]
            return carry

        lax.fori_loop(0, length // block, step, 0)

    def fetch(self):
        for i, (at, row, height, col, width) in enumerate(self.chunks):
            t = self.begin[i]
            if 1 <= t <= self.bits:
                start, length = self.regions[i][t - 1]
                own = pl.ds(pl.multiple_of(self.core * (self.shapes[at][1] // 2) + col, 128), width)
                self.loads[i] = pltpu.make_async_copy(
                    self.sources[at].at[span(row + start, length), own],
                    self.acc[i].at[span(start, length)],
                    self.load_sem.at[i],
                )
                self.loads[i].start()

    def arrived(self, i, t):
        if (i, t) in self.live:
            self.live[i, t].wait_recv()

    def task(self, i, t):
        at, row, height, col, width = self.chunks[i]
        bits, kinds, regions, stages = self.bits, self.kinds[i], self.regions[i], self.stages[i]
        half = self.shapes[at][1] // 2
        own = pl.ds(pl.multiple_of(self.core * half + col, 128), width)
        rows = pl.ds(row, height)
        if t == 0:
            away = pl.ds(pl.multiple_of((1 - self.core) * half + col, 128), width)
            self.send(i, 0, self.sources[at].at[rows, away], self.recv0[i], self.sibling)
            if self.acc[i] is None:
                self.acc[i] = self.sources[at].at[rows, own]
                return
            copy = pltpu.make_async_copy(self.sources[at].at[rows, own], self.acc[i], self.load_sem.at[i])
            copy.start()
            self.loads[i] = copy
            return
        self.arrived(i, t - 1)
        if t <= bits + 1:
            if t == self.begin[i]:
                if t <= bits:
                    self.loads[i].wait()
            elif t == 1:
                if i in self.loads:
                    self.loads[i].wait()
                self.add(self.acc[i], 0, self.recv0[i], 0, height)
            else:
                s = t - 2
                start, length = regions[s + 1]
                if not kinds[s]:
                    self.live[i, t - 1].wait_send()
                self.add(self.acc[i], start, self.recvs[i], self.slots[i][s], length)
        if t == self.leave[i]:
            start, length = regions[t - 1]
            copy = pltpu.make_async_copy(
                self.acc[i].at[span(start, length)], self.outs[at].at[span(row + start, length), own], self.store_sem.at[i]
            )
            copy.start()
            self.stores[i] = copy
            return
        if t <= bits:
            s = t - 1
            start, length = regions[s]
            give, first = length, start
            if kinds[s]:
                give = length // 2
                first = start + (1 - stages[s][0]) * give
            self.send(
                i, t, self.acc[i].at[span(first, give)], self.recvs[i].at[pl.ds(self.slots[i][s], give)],
                (stages[s][1], self.core),
            )
            return
        if t == bits + 1:
            start, length = regions[bits]
            if t == self.begin[i]:
                mine = self.sources[at].at[span(row + start, length), own]
            else:
                mine = self.acc[i].at[span(start, length)]
            copy = pltpu.make_async_copy(mine, self.outs[at].at[span(row + start, length), own], self.store_sem.at[i])
            copy.start()
            self.stores[i] = copy
        if t == bits + 2:
            self.stores[i].wait()
        if t <= 2 * bits:
            s = bits - 1 - (t - bits - 1)
            start, length = regions[s + 1]
            if kinds[s]:
                place = self.outs[at].at[span(row + start, length), own]
                self.send(i, t, mine if t == bits + 1 else place, place, (stages[s][1], self.core))
            return
        if t == 2 * bits + 1:
            place = self.outs[at].at[rows, own]
            self.send(i, t, place, place, self.sibling)

    def run(self, order):
        while self.at < len(order):
            token = order[self.at]
            self.at += 1
            if token is None:
                return
            i, t = token
            if t == self.total:
                self.arrived(i, t - 1)
            else:
                self.task(i, t)

    def finish(self):
        for (i, t), copy in self.live.items():
            if not (1 <= t <= self.bits and not self.kinds[i][t - 1]):
                copy.wait_send()


def share_scratch(chunks, bits, begin, inside=False):
    acc, recv0, recvs = [], [], []
    for i, (at, row, height, col, width) in enumerate(chunks):
        if begin[i] > bits:
            continue
        acc.append(pltpu.VMEM((height, width), BF16))
        if begin[i] == 0:
            recv0.append(pltpu.VMEM((height, width), BF16))
        length, used = height, 0
        for s in range(bits):
            if length % 32 == 0:
                length //= 2
            used += length
        recvs.append(pltpu.VMEM((used, width), BF16))
    n = len(chunks)
    sems = [pltpu.SemaphoreType.DMA((n, 2 * bits + 2))] * 2 + [pltpu.SemaphoreType.DMA((n,))] * 2
    return ([] if inside else acc) + recv0 + recvs + sems


def share_hold(refs, bits, begin, inside=False):
    n = len(begin)
    acc, recv0, recvs = [None] * n, [None] * n, [None] * n
    for held, most in ((acc, -1 if inside else bits), (recv0, 0), (recvs, bits)):
        for i in range(n):
            if begin[i] <= most:
                held[i], refs = refs[0], refs[1:]
    return acc, recv0, recvs, refs


def share_leave(bits):
    return [bits + 1] * 3 + [min(3, bits + 1)] * 3


def share_orders(bits, path):
    rest = list(range(2, bits))
    if bits < 2:
        return rest or list(range(bits)), rest or list(range(bits))
    if path == 0:
        return [0, 1] + rest, [1, 0] + rest
    if path == 1:
        return [0] + rest + [1], [1] + rest + [0]
    return rest + [0, 1], rest + [1, 0]


SHARE_CUTS = ((1, 2), (1, 1), (3, 1), (1, 1), (1, 1), (1, 1), (1, 1))
SHARE_FIRST = 6
SHARE_PATHS = (0, 1, 1, 0, 1, 0, 0, 0, 0, 0)
SHARE_LATE = (
    21, 51, 96, 83, 5, 37, -1, 97, -1, 22, 52, 6, -1, 98, -1, -1, -1, 53, -1, 23, 112, 84, 7, -1,
    54, -1, 113, 8, 67, -1, -1, 55, 85, -1, 114, -1, 24, 99, 38, -1, 128, 86, 68, -1, 56, 115, 9, -1,
    129, 69, -1, 116, 39, 100, -1, 10, -1, -1, 117, 144, 87, 25, 101, 118, 145, 57, 70, 130, 26, 88, 40, 102,
    146, 58, 131, 119, 71, 147, 103, 120, 132, 148, 104, 133, 149, 89, 72, 121, 41, 150, 134, 122, 90, 151, 105, 42,
    135, 73, 152, 106, 136, 74, 153, 154, 137, 138,
)
SHARE_EARLY = (
    32, -1, 33, 16, -1, -1, 17, 0, -1, 34, -1, 1, -1, 18, -1, 48, -1, -1, 35, -1, 64, 49, 2, -1,
    65, 80, 19, -1, -1, 81, 3, 36, -1, -1, 66, 20, 37, 50, 4, -1, 82, -1, 21, 5, 51, 83, 67,
)


def share_late_order(pieces, bits, parts, ready):
    if bits == 4:
        return [None if v < 0 else (v // 16, v % 16) for v in SHARE_LATE]
    order, total = [], 2 * bits + 2
    begin = share_leave(bits) + [0] * (pieces - SHARE_FIRST)
    for k in range(parts + total + 1):
        for i in range(pieces):
            t = k - ready[i] + begin[i]
            if k >= ready[i] and t <= total:
                order.append((i, t))
        if k < parts:
            order.append(None)
    return order


def share_early_order(bits):
    if bits == 4:
        return [None if v < 0 else (v // 16, v % 16) for v in SHARE_EARLY]
    order = [None] * 10
    for t in range(bits + 2):
        order += [(i, t) for i in range(SHARE_FIRST) if t <= share_leave(bits)[i]] + [None]
    return order


def meet_sums(links, e, width, tables, between=None):
    links.wait_near(e)
    links.far[e][links.outer] = fold_sums(links.near[e], links.wide)
    links.send_far(e)
    if between is not None:
        between()
    links.wait_far(e)
    sums = fold_sums(links.far[e], links.outers)
    for t, (table, row) in enumerate(tables):
        unpack(table, row, sums[8 * t : 8 * t + 8], width)


def share_of(wv, tally, crop, times):
    return wv[0, crop] * (times / tally[0:1, 0:1]) + wv[1, crop] * (times / tally[1:2, 0:1])


class Puts:
    def __init__(self, sem):
        self.sem, self.copies = sem, []

    def put(self, src, dst):
        copy = pltpu.make_async_copy(src, dst, self.sem.at[len(self.copies)])
        copy.start()
        self.copies.append(copy)

    def finish(self):
        for copy in self.copies:
            copy.wait()


def start_loads(pairs, sem):
    copies = [pltpu.make_async_copy(src, dst, sem.at[i]) for i, (src, dst) in enumerate(pairs)]
    for copy in copies:
        copy.start()
    return copies


def back_two_kernel(sets, total, outs, crops, dims, shapes, chunks, *refs):
    c3, cin, c4, cout = dims
    vb, vs, norms1, norms2, st3, st4, st5, tally = refs[:8]
    sources, refs = refs[8:23], refs[23:]
    (o_up, o_g6, o_g7, o_g5, o_g4, o_s5, o_s4, o_s3), refs = refs[:8], refs[8:]
    held, refs = refs[:14], refs[14:]
    (d6, w6, z5, h5, d7, xe, w7, w5, x5, z4, w4, h2, w3, img) = held
    (q5, t7, dh, d4, zt, bg, up, s5, s4, s3, cs, cm, wv, wcol), refs = refs[:14], refs[14:]
    d5, pv, blk = d6, q5, img
    g6, g7, g5, g4 = w6, w7, w5, w4
    blocks, refs = take(refs, 3)
    near, refs = take(refs, 3)
    far, refs = take(refs, 3)
    links = Links(crops, near, far, *refs[:4])
    load_sem, out_sem, up_sem = refs[4:7]
    refs = refs[7:]
    bits = crops.bit_length() - 1
    early = SHARE_FIRST
    acc, recv0, recvs, refs = share_hold(refs, bits, [0] * early, True)
    share = Share(
        shapes, chunks[:early], [share_orders(bits, v) for v in SHARE_PATHS[:early]], bits, links, [g7, g6, g5], [o_g7, o_g6, o_g5],
        acc, recv0, recvs, refs, [0] * early, share_leave(bits),
    )
    order = share_early_order(bits)

    def tick():
        share.run(order)

    f = F32
    loads = start_loads(list(zip(sources, held)), load_sem)
    links.greet()
    view_tables(sets, links.r, (vb, vs), wv, wcol)
    puts = Puts(out_sem)
    for ref in (cs, cm):
        ref[...] = jnp.zeros(ref.shape, f)
    for block in blocks:
        block[...] = jnp.zeros(block.shape, f)

    for i in range(3):
        loads[i].wait()
    q5[...] = mm_nt(d6[...], w6[...])
    g5at = c4
    for m in sets:

        def crop_(c, m=m):
            crop = m.crop0 + c
            rows = span(m.out0 + c * m.out, m.out, 8)
            inv = by_view(wv, crop, st5[2:4, :])
            n = (z5[rows, :] - by_view(wv, crop, st5[0:2, :])) * inv
            q = act_slope(n * norms2[0:1, g5at : 2 * c4] + norms2[1:2, g5at : 2 * c4]) * q5[rows, :]
            q5[rows, :] = q
            cs[pl.ds(crop, 1), 0:c4] = jnp.sum(tile_sum(q), axis=0, keepdims=True)
            cm[pl.ds(crop, 1), 0:c4] = jnp.sum(tile_sum(q * n), axis=0, keepdims=True)

        repeat(m.count, crop_)
    local_sums(blocks[0], (cs, cm), wcol, c4)
    links.send_near(0, blocks[0])

    loads[3].wait()

    def outer(n):
        cols = pl.ds(pl.multiple_of(n * 512, 512), 512)
        g6[:, cols] = mm_tn(h5[...], d6[:, cols]).astype(BF16)

    repeat(cout // 512, outer)
    tick()

    def rest():
        for i in (4, 5, 6):
            loads[i].wait()

        def shortcut(n):
            part = pl.ds(pl.multiple_of(n * 256, 256), 256)
            t7[:, part] = mm_nt(d7[...], w7[part, :])

        repeat(cin // 256, shortcut)

        def skip(n):
            cols = pl.ds(pl.multiple_of(n * 512, 512), 512)
            g7[:, cols] = mm_tn(xe[...], d7[:, cols]).astype(BF16)

        repeat(cout // 512, skip)
        tick()

    meet_sums(links, 0, c4, ((s5, 0), (s5, 2)), rest)

    for m in sets:

        def pair(p, m=m):
            o = m.out0 + p * 2 * m.out
            mask = keep(c4, 8, m.half)
            slots = [[], [], [], []]
            for j in range(2):
                crop = m.crop0 + 2 * p + j
                rows = span(o + j * m.out, m.out, 8)
                over = share_of(wv, tally, crop, 4.0)
                inv = by_view(wv, crop, st5[2:4, :])
                n = (z5[rows, :] - by_view(wv, crop, st5[0:2, :])) * inv
                d = (inv * norms2[0:1, g5at : 2 * c4]) * (
                    q5[rows, :] - by_view(wv, crop, s5[0:2, :]) * over - n * (by_view(wv, crop, s5[2:4, :]) * over)
                )
                d = masked(d, mask)
                down = jnp.concatenate([d[8:], jnp.zeros((8, c4), f)], axis=0)
                slots[0].append(d)
                slots[1].append(pltpu.roll(d, m.out - 1, 0))
                slots[2].append(down)
                slots[3].append(pltpu.roll(down, m.out - 1, 0))
            for t in range(4):
                d5[span(o, 2 * m.out), t * c4 : (t + 1) * c4] = jnp.concatenate(slots[t], axis=0).astype(BF16)

        repeat(m.count // 2, pair)

    tick()
    loads[7].wait()
    options = (((1, 0),), ((2, 0), (0, 1)))
    for a in range(2):
        for b in range(2):
            value = None
            for r, down in options[a]:
                for c, side in options[b]:
                    slot, tap = (2 * down + side) * c4, (3 * r + c) * c4
                    term = mm_nt(d5[:, slot : slot + c4], w5[tap : tap + c4, :])
                    value = term if value is None else value + term
            pv[...] = value
            for m in sets:

                def crop_(c, m=m, a=a, b=b):
                    for i in range(m.half):
                        for q in range(c4 // 128):
                            dh[q, pl.ds(m.row0 + c * m.rows + (2 * i + a) * 16 + b, 8, stride=2), :] = pv[
                                span(m.out0 + c * m.out + i * 8, 8, 8), q * 128 : (q + 1) * 128
                            ]

                repeat(m.count, crop_)
        tick()
    loads[9].wait()
    for m in sets:

        def crop_(c, m=m):
            crop = m.crop0 + c
            rows = span(m.row0 + c * m.rows, m.rows)
            mask = keep(128, 16, m.edge)
            levels, tilts = [], []
            for q in range(c4 // 128):
                cols = slice(q * 128, (q + 1) * 128)
                inv = by_view(wv, crop, st4[2:4, cols])
                n = (z4[rows, cols] - by_view(wv, crop, st4[0:2, cols])) * inv
                up_ = masked(act_slope(n * norms2[0:1, cols] + norms2[1:2, cols]) * dh[q, rows, :], mask)
                dh[q, rows, :] = up_
                levels.append(jnp.sum(tile_sum(up_), axis=0, keepdims=True))
                tilts.append(jnp.sum(tile_sum(up_ * n), axis=0, keepdims=True))
            cs[pl.ds(crop, 1), 0:c4] = jnp.concatenate(levels, axis=1)
            cm[pl.ds(crop, 1), 0:c4] = jnp.concatenate(tilts, axis=1)

        repeat(m.count, crop_)
        tick()
    local_sums(blocks[1], (cs, cm), wcol, c4)
    links.send_near(1, blocks[1])
    loads[8].wait()

    def kernel(n):
        for t in range(3 * n, 3 * n + 3):
            part = slice(t * c4, (t + 1) * c4)
            g5[part, :] = mm_tn(x5[:, part], d5[:, 0:c4]).astype(BF16)
        tick()

    kernel(0)

    def rest():
        kernel(1)
        kernel(2)

    meet_sums(links, 1, c4, ((s4, 0), (s4, 2)), rest)
    tick()

    for i in range(10, 14):
        loads[i].wait()
    big_rows = 2 * sets[0].rows
    for at, m in enumerate(sets):

        def pair(p, m=m, at=at):
            r = m.row0 + p * 2 * m.rows
            o = m.out0 + p * 2 * m.out
            mask = keep(128, 16, m.edge)
            for j in range(2):
                crop = m.crop0 + 2 * p + j
                rows = span(r + j * m.rows, m.rows)
                over = share_of(wv, tally, crop, 1.0)
                for q in range(c4 // 128):
                    cols = slice(q * 128, (q + 1) * 128)
                    inv = by_view(wv, crop, st4[2:4, cols])
                    n = (z4[rows, cols] - by_view(wv, crop, st4[0:2, cols])) * inv
                    d = (inv * norms2[0:1, cols]) * (
                        dh[q, rows, :] - by_view(wv, crop, s4[0:2, cols]) * over - n * (by_view(wv, crop, s4[2:4, cols]) * over)
                    )
                    d4[rows, cols] = masked(d, mask).astype(BF16)
            got = mm_nt(d4[span(r, 2 * m.rows), :], w4[...])
            for q in range(cin // 128):
                bg[q, 0 : 2 * m.rows, :] = got[:, q * 128 : (q + 1) * 128]
            for q in range(cin // 128):
                for j in range(2):
                    for i in range(m.half):
                        here = pl.ds(j * m.rows + i * 32, 8, stride=2)
                        bg[q, here, :] = bg[q, here, :] + t7[span(o + j * m.out + i * 8, 8, 8), q * 128 : (q + 1) * 128]
            turn = m.crop0 // 2 + p
            slot = turn % 2

            def left(turn, slot):
                return pltpu.make_async_copy(
                    up.at[slot, 0 : 2 * m.rows], o_up.at[span(r, 2 * m.rows)], up_sem.at[turn]
                )

            if turn >= 2:
                size = big_rows if turn - 2 < sets[0].count // 2 else 2 * m.rows
                pltpu.make_async_copy(up.at[slot, 0:size], o_up.at[pl.ds(0, size)], up_sem.at[turn - 2]).wait()
            step = m.rows // 2
            mask = keep(128, 16, m.edge)
            totals = [[[], []], [[], []]]
            for h, j in [(h, j) for h in range(cin // 512) for j in range(2)]:
                if j == 0:
                    zt[0 : 2 * m.rows, :] = mm(h2[span(r, 2 * m.rows), :], w3[:, h * 512 : (h + 1) * 512])
                crop = m.crop0 + 2 * p + j
                levels, tilts = totals[j]
                for q in range(h * 4, h * 4 + 4):
                    cols = slice(q * 128, (q + 1) * 128)
                    part = slice((q - h * 4) * 128, (q - h * 4 + 1) * 128)
                    at3 = slice(2 * c3 + q * 128, 2 * c3 + (q + 1) * 128)
                    mean, inv = by_view(wv, crop, st3[0:2, cols]), by_view(wv, crop, st3[2:4, cols])
                    gain, bias = norms1[0:1, at3], norms1[1:2, at3]

                    def tile(i, sums, j=j, cols=cols, part=part, q=q, mean=mean, inv=inv, gain=gain, bias=bias):
                        here = span(j * m.rows + i * step, step)
                        rows = span(r + j * m.rows + i * step, step)
                        n = (zt[here, part] - mean) * inv
                        u = n * gain + bias + img[rows, cols].astype(f)
                        got = bg[q, here, :].astype(BF16).astype(f)
                        v = masked(act_slope(u) * got, mask)
                        up[slot, here, cols] = v
                        return (sums[0] + tile_sum(v), sums[1] + tile_sum(v * n))

                    zero = jnp.zeros((8, 128), f)
                    s, t = lax.fori_loop(0, 2, tile, (zero, zero))
                    levels.append(jnp.sum(s, axis=0, keepdims=True))
                    tilts.append(jnp.sum(t, axis=0, keepdims=True))
            for j in range(2):
                crop = m.crop0 + 2 * p + j
                cs[pl.ds(crop, 1), :] = jnp.concatenate(totals[j][0], axis=1)
                cm[pl.ds(crop, 1), :] = jnp.concatenate(totals[j][1], axis=1)
            left(turn, slot).start()

        for p in range(m.count // 2):
            pair(p)
            tick()
    late = pltpu.make_async_copy(sources[14], blk, load_sem.at[14])
    late.start()
    local_sums(blocks[2], (cs, cm), wcol, cin)
    links.send_near(2, blocks[2])
    late.wait()

    def inner(n):
        part = pl.ds(pl.multiple_of(n * 256, 256), 256)
        g4[part, :] = mm_tn(blk[:, part], d4[...]).astype(BF16)

    repeat(2, inner)
    tick()

    def rest():
        repeat(cin // 256 - 2, lambda n: inner(n + 2))
        puts.put(g4, o_g4)
        tick()

    meet_sums(links, 2, cin, ((s3, 0), (s3, 2)), rest)
    for src, dst in ((s5, o_s5), (s4, o_s4), (s3, o_s3)):
        puts.put(src, dst)
    for back in (2, 1):
        size = 2 * sets[1].rows
        turn = (sets[0].count + sets[1].count) // 2 - back
        pltpu.make_async_copy(
            up.at[turn % 2, 0:size], o_up.at[pl.ds(sets[1].row0, size)], up_sem.at[turn]
        ).wait()
    while share.at < len(order):
        tick()
    for copy in share.stores.values():
        copy.wait()
    share.finish()
    links.finish()
    puts.finish()


def back_one_kernel(sets, total, guarded, crops, dims, shapes, chunks, *refs):
    c3, cin = dims
    vb, vs, norms1, st1, st2, st3, s3, tally = refs[:8]
    sources, refs = refs[8:17], refs[17:]
    second, refs = list(refs[:4]), refs[4:]
    (o_gb, o_gs, o_s2, o_s1), refs = refs[:4], refs[4:]
    o_grads, refs = refs[:7], refs[7:]
    held, refs = refs[:9], refs[9:]
    (h2, w3, up, z2, h1, wsp1, z1, w1, img) = held
    (zt, d3, q2, d2, q1, d1, g3, g2, g1, s2, s1, cs, cm, wv, wcol), refs = refs[:15], refs[15:]
    blocks, refs = take(refs, 2)
    near, refs = take(refs, 2)
    far, refs = take(refs, 2)
    links = Links(crops, near, far, *refs[:4])
    load_sem, out_sem, own_sem, grad_send, grad_recv, up_sem = refs[4:10]
    refs = refs[10:]
    n = len(chunks)
    bits = crops.bit_length() - 1
    begin = share_leave(bits) + [0] * (n - SHARE_FIRST)
    acc, recv0, recvs, refs = share_hold(refs, bits, begin)
    share = Share(
        shapes, chunks, [share_orders(bits, v) for v in SHARE_PATHS], bits, links, second + [g3, g2, g1], o_grads,
        acc, recv0, recvs, refs, begin, [2 * bits + 3] * n,
    )
    share.fetch()
    order = share_late_order(n, bits, 20, (0,) * 7 + (7, 14, 20))

    def tick():
        share.run(order)

    core = links.r
    sibling = (links.k, 1 - core)
    f = F32
    loads = start_loads([(a, b) for a, b in zip(sources, held) if b is not up], load_sem)
    ups = []
    for m in sets:
        for p in range(m.count // 2):
            rows = pl.ds(m.row0 + p * 2 * m.rows, 2 * m.rows)
            ups.append(pltpu.make_async_copy(sources[2].at[rows], up.at[rows], up_sem.at[len(ups)]))
    for copy in ups:
        copy.start()
    links.greet()
    tick()
    view_tables(sets, links.r, (vb, vs), wv, wcol)
    puts = Puts(out_sem)
    for ref in (cs, cm):
        ref[...] = jnp.zeros(ref.shape, f)
    for block in blocks:
        block[...] = jnp.zeros(block.shape, f)
    d2[0:16, :] = jnp.zeros((16, 3 * c3), BF16)
    for m in sets:
        for c in range(m.count):
            at = m.guard0 + c * m.guard + m.rows
            d2[at : at + 16, :] = jnp.zeros((16, 3 * c3), BF16)

    for i in range(3):
        loads[i].wait()
    for copy in ups:
        copy.wait()
    for m in sets:

        def pair(p, m=m):
            r = m.row0 + p * 2 * m.rows
            step = m.rows // 2
            mask = keep(128, 16, m.edge)
            for h, j in [(h, j) for h in range(cin // 512) for j in range(2)]:
                if j == 0:
                    zt[0 : 2 * m.rows, :] = mm(h2[span(r, 2 * m.rows), :], w3[:, h * 512 : (h + 1) * 512])
                crop = m.crop0 + 2 * p + j
                over = share_of(wv, tally, crop, 1.0)
                for q in range(h * 4, h * 4 + 4):
                    cols = slice(q * 128, (q + 1) * 128)
                    part = slice((q - h * 4) * 128, (q - h * 4 + 1) * 128)
                    mean, inv = by_view(wv, crop, st3[0:2, cols]), by_view(wv, crop, st3[2:4, cols])
                    gain = inv * norms1[0:1, 2 * c3 + q * 128 : 2 * c3 + (q + 1) * 128]
                    level = by_view(wv, crop, s3[0:2, cols]) * over
                    tilt = by_view(wv, crop, s3[2:4, cols]) * over * inv

                    def tile(i, j=j, cols=cols, part=part, mean=mean, gain=gain, level=level, tilt=tilt):
                        here = span(j * m.rows + i * step, step)
                        rows = span(r + j * m.rows + i * step, step)
                        d = gain * (up[rows, cols] - level - (zt[here, part] - mean) * tilt)
                        d3[rows, cols] = masked(d, mask).astype(BF16)

                    repeat(2, tile)
            q2[span(r, 2 * m.rows), :] = mm_nt(d3[span(r, 2 * m.rows), :], w3[...])
            for j in range(2):
                crop = m.crop0 + 2 * p + j
                mean, inv = by_view(wv, crop, st2[0:2, :]), by_view(wv, crop, st2[2:4, :])

                def tile(i, sums, j=j, mean=mean, inv=inv):
                    rows = span(r + j * m.rows + i * step, step)
                    n = (z2[rows, :] - mean) * inv
                    v = act_slope(n * norms1[0:1, c3 : 2 * c3] + norms1[1:2, c3 : 2 * c3]) * q2[rows, :]
                    q2[rows, :] = v
                    return (sums[0] + tile_sum(v), sums[1] + tile_sum(v * n))

                zero = jnp.zeros((8, c3), f)
                s, t = lax.fori_loop(0, 2, tile, (zero, zero))
                cs[pl.ds(crop, 1), 0:c3] = jnp.sum(s, axis=0, keepdims=True)
                cm[pl.ds(crop, 1), 0:c3] = jnp.sum(t, axis=0, keepdims=True)

        for p in range(m.count // 2):
            pair(p)
            tick()
    local_sums(blocks[0], (cs, cm), wcol, c3)
    links.send_near(0, blocks[0])

    def outer(n):
        cols = pl.ds(pl.multiple_of(n * 256, 256), 256)
        g3[:, cols] = mm_tn(h2[...], d3[:, cols]).astype(BF16)

    repeat(cin // 512, outer)
    tick()

    def rest():
        repeat(cin // 512, lambda n: outer(n + cin // 512))
        tick()

    meet_sums(links, 0, c3, ((s2, 0), (s2, 2)), rest)

    for i in range(3, 6):
        loads[i].wait()
    for m in sets:

        def pair(p, m=m):
            r = m.row0 + p * 2 * m.rows
            g = m.guard0 + p * 2 * m.guard
            step = m.rows // 2
            mask = keep(c3, 16, m.edge)
            for j in range(2):
                crop = m.crop0 + 2 * p + j
                over = share_of(wv, tally, crop, 1.0)
                mean, inv = by_view(wv, crop, st2[0:2, :]), by_view(wv, crop, st2[2:4, :])
                gain = inv * norms1[0:1, c3 : 2 * c3]
                level = by_view(wv, crop, s2[0:2, :]) * over
                tilt = by_view(wv, crop, s2[2:4, :]) * over * inv

                def tile(i, j=j, mean=mean, gain=gain, level=level, tilt=tilt):
                    rows = span(r + j * m.rows + i * step, step)
                    d = gain * (q2[rows, :] - level - (z2[rows, :] - mean) * tilt)
                    d = masked(d, mask)
                    to = span(g + j * m.guard + i * step, step)
                    d2[to, 0:c3] = pltpu.roll(d, step - 1, 0).astype(BF16)
                    d2[to, c3 : 2 * c3] = d.astype(BF16)
                    d2[to, 2 * c3 : 3 * c3] = pltpu.roll(d, 1, 0).astype(BF16)

                repeat(2, tile)
            size = 2 * m.rows + 16
            value = None
            for a in range(3):
                for b in range(3):
                    part = d2[span(g - (a - 1) * 16, size), b * c3 : (b + 1) * c3]
                    term = mm_nt(part, wsp1[a, b * c3 : (b + 1) * c3, :])
                    value = term if value is None else value + term
            q1[span(r, m.rows), :] = value[0 : m.rows]
            q1[span(r + m.rows, m.rows), :] = value[m.guard : m.guard + m.rows]
            for j in range(2):
                crop = m.crop0 + 2 * p + j
                mean, inv = by_view(wv, crop, st1[0:2, :]), by_view(wv, crop, st1[2:4, :])

                def tile(i, sums, j=j, mean=mean, inv=inv):
                    rows = span(r + j * m.rows + i * step, step)
                    n = (z1[rows, :] - mean) * inv
                    v = act_slope(n * norms1[0:1, 0:c3] + norms1[1:2, 0:c3]) * q1[rows, :]
                    v = masked(v, mask)
                    q1[rows, :] = v
                    return (sums[0] + tile_sum(v), sums[1] + tile_sum(v * n))

                zero = jnp.zeros((8, c3), f)
                s, t = lax.fori_loop(0, 2, tile, (zero, zero))
                cs[pl.ds(crop, 1), 0:c3] = jnp.sum(s, axis=0, keepdims=True)
                cm[pl.ds(crop, 1), 0:c3] = jnp.sum(t, axis=0, keepdims=True)

        for p in range(m.count // 2):
            pair(p)
            tick()
    local_sums(blocks[1], (cs, cm), wcol, c3)
    links.send_near(1, blocks[1])
    inside = guarded - 32

    def taps(a):
        g2[a * 3 * c3 : (a + 1) * 3 * c3, :] = mm_tn(
            h1[a * 16 : a * 16 + inside, :], d2[16 : 16 + inside, c3 : 2 * c3]
        ).astype(BF16)

    taps(0)
    tick()

    def rest():
        taps(1)
        taps(2)
        tick()

    meet_sums(links, 1, c3, ((s1, 0), (s1, 2)), rest)

    loads[6].wait()
    moves = []
    for m, out in zip(sets, (o_gb, o_gs)):
        part = m.rows // 2
        for c in range(m.count):
            i = m.crop0 + c
            own_rows = span(m.row0 + c * m.rows + core * part, part)
            other_rows = span(m.row0 + c * m.rows + (1 - core) * part, part)
            place = out.at[span((core * m.count + c) * part, part)]
            moves.append(
                (
                    pltpu.make_async_copy(d3.at[own_rows], place, own_sem.at[i]),
                    pltpu.make_async_remote_copy(
                        src_ref=d3.at[other_rows],
                        dst_ref=place,
                        send_sem=grad_send.at[i],
                        recv_sem=grad_recv.at[i],
                        device_id=sibling,
                        device_id_type=MESH,
                    ),
                )
            )
    for m in sets:

        def pair(p, m=m):
            r = m.row0 + p * 2 * m.rows
            step = m.rows // 2
            mask = keep(c3, 16, m.edge)
            for j in range(2):
                crop = m.crop0 + 2 * p + j
                over = share_of(wv, tally, crop, 1.0)
                mean, inv = by_view(wv, crop, st1[0:2, :]), by_view(wv, crop, st1[2:4, :])
                gain = inv * norms1[0:1, 0:c3]
                level = by_view(wv, crop, s1[0:2, :]) * over
                tilt = by_view(wv, crop, s1[2:4, :]) * over * inv

                def tile(i, j=j, mean=mean, gain=gain, level=level, tilt=tilt):
                    rows = span(r + j * m.rows + i * step, step)
                    d = gain * (q1[rows, :] - level - (z1[rows, :] - mean) * tilt)
                    d1[rows, :] = masked(d, mask).astype(BF16)

                repeat(2, tile)
            rows = span(r, 2 * m.rows)
            for n in range(cin // 256):
                cols = slice(n * 256, (n + 1) * 256)
                d3[rows, cols] = (up[rows, cols] + mm_nt(d1[rows, :], w1[cols, :])).astype(BF16)

        for p in range(m.count // 2):
            pair(p)
            for c in (2 * p, 2 * p + 1):
                for copy in moves[m.crop0 + c]:
                    copy.start()
            tick()
    loads[7].wait()

    def inner(n):
        part = pl.ds(pl.multiple_of(n * 256, 256), 256)
        g1[part, :] = mm_tn(img[:, part], d1[...]).astype(BF16)

    repeat(cin // 256, inner)
    for src, dst in ((s2, o_s2), (s1, o_s1)):
        puts.put(src, dst)
    while share.at < len(order):
        tick()
    share.finish()
    links.finish()
    for near_copy, far_copy in moves:
        near_copy.wait()
        far_copy.wait()
    puts.finish()


def backward(sets, got, views, w, norms_first, norms_second, total, guarded, outs, idents):
    crops = lax.axis_size("crops")
    w1, wsp1, w3, w4, w5, w6, w7 = w
    cin, c3 = w1.shape
    c4, cout = w6.shape
    (
        f_img, f_z1, f_h1, f_z2, f_h2, f_blk, f_z4, f_x5, f_z5, f_h5, f_xe, f_res, f_d6, f_d7,
        f_st1, f_st2, f_st3, f_st4, f_st7, f_st5, f_st6, f_sq, f_n,
    ) = got
    smem, vmem = pl.BlockSpec(memory_space=pltpu.SMEM), pl.BlockSpec(memory_space=pltpu.VMEM)
    hbm = pl.BlockSpec(memory_space=pl.ANY)
    shape = jax.ShapeDtypeStruct
    most = 2 * sets[0].rows
    pairs = sum(m.count for m in sets) // 2
    count = 2 * pairs

    def like(arrays):
        return [pltpu.VMEM(t.shape, t.dtype) for t in arrays]

    def params(ident):
        return pltpu.CompilerParams(
            collective_id=ident, has_side_effects=True, vmem_limit_bytes=63 * 1024 * 1024
        )

    arrays = [f_d6, w6, f_z5, f_h5, f_d7, f_xe, w7, w5, f_x5, f_z4, w4, f_h2, w3, f_img, f_blk]
    out_shape = [
        shape((total, cin), F32), shape((c4, cout), BF16), shape((cin, cout), BF16), shape((9 * c4, c4), BF16),
        shape((cin, c4), BF16), shape((8, c4), F32), shape((8, c4), F32), shape((8, cin), F32),
    ]
    scratch = like(arrays[:14]) + [
        pltpu.VMEM((outs, c4), F32), pltpu.VMEM((outs, cin), F32), pltpu.VMEM((c4 // 128, total, 128), F32), pltpu.VMEM((total, c4), BF16),
        pltpu.VMEM((most, 512), F32), pltpu.VMEM((cin // 128, most, 128), F32), pltpu.VMEM((2, most, cin), F32),
        pltpu.VMEM((8, c4), F32), pltpu.VMEM((8, c4), F32), pltpu.VMEM((8, cin), F32),
        pltpu.VMEM((16, cin), F32), pltpu.VMEM((16, cin), F32),
        pltpu.SMEM((2, 16), F32), pltpu.VMEM((16, 128), F32),
    ]
    scratch += exchange_shapes((c4, c4, cin), (2, 2, 2), crops)
    scratch += [pltpu.SemaphoreType.DMA((15,)), pltpu.SemaphoreType.DMA((7,)), pltpu.SemaphoreType.DMA((pairs,))]
    shapes = [(cin, cout), (c4, cout), (9 * c4, c4), (cin, c4), (c3, cin), (9 * c3, c3), (cin, c3)]
    chunks = share_plan(shapes, SHARE_CUTS)
    bits = crops.bit_length() - 1
    scratch += share_scratch(chunks[:SHARE_FIRST], bits, [0] * SHARE_FIRST, True)
    up, g_outer2, g_skip, g_spatial2, g_inner2, s5, s4, s3 = pl.pallas_call(
        functools.partial(back_two_kernel, sets, total, outs, crops, (c3, cin, c4, cout), shapes, chunks),
        out_shape=out_shape,
        in_specs=[smem] * 2 + [vmem] * 6 + [hbm] * 15,
        out_specs=[hbm] * len(out_shape),
        scratch_shapes=scratch,
        compiler_params=params(idents[0]),
        name="back_two",
    )(*views, norms_first, norms_second, f_st3, f_st4, f_st5, f_n, *arrays)

    arrays = [f_h2, w3, up, f_z2, f_h1, wsp1, f_z1, w1, f_img]
    out_shape = [
        shape((total_rows(sets[0]), cin), BF16), shape((total_rows(sets[1]), cin), BF16), shape((8, c3), F32),
        shape((8, c3), F32),
    ] + [shape(t, BF16) for t in shapes]
    scratch = like(arrays) + [
        pltpu.VMEM((most, 512), F32), pltpu.VMEM((total, cin), BF16), pltpu.VMEM((total, c3), F32),
        pltpu.VMEM((guarded, 3 * c3), BF16), pltpu.VMEM((total, c3), F32), pltpu.VMEM((total, c3), BF16),
        pltpu.VMEM((c3, cin), BF16), pltpu.VMEM((9 * c3, c3), BF16), pltpu.VMEM((cin, c3), BF16),
        pltpu.VMEM((8, c3), F32), pltpu.VMEM((8, c3), F32), pltpu.VMEM((16, c3), F32), pltpu.VMEM((16, c3), F32),
        pltpu.SMEM((2, 16), F32), pltpu.VMEM((16, 128), F32),
    ]
    scratch += exchange_shapes((c3, c3), (2, 2), crops)
    scratch += [pltpu.SemaphoreType.DMA((9,)), pltpu.SemaphoreType.DMA((2,))]
    scratch += [pltpu.SemaphoreType.DMA((count,))] * 3 + [pltpu.SemaphoreType.DMA((pairs,))]
    scratch += share_scratch(chunks, bits, share_leave(bits) + [0] * (len(chunks) - SHARE_FIRST))
    grad_b, grad_s, s2, s1, *grads = pl.pallas_call(
        functools.partial(back_one_kernel, sets, total, guarded, crops, (c3, cin), shapes, chunks),
        out_shape=out_shape,
        in_specs=[smem] * 2 + [vmem] * 6 + [hbm] * 13,
        out_specs=[hbm] * len(out_shape),
        scratch_shapes=scratch,
        compiler_params=params(idents[1]),
        name="back_one",
    )(*views, norms_first, f_st1, f_st2, f_st3, s3, f_n, *arrays, g_skip, g_outer2, g_spatial2, g_inner2)
    return grad_b, grad_s, grads, (s1, s2, s3, s4, s5)


def widen_kernel(*refs):
    for src, dst in zip(refs[: len(refs) // 2], refs[len(refs) // 2 :]):
        dst[...] = src[...].astype(F32)


def widen(arrays, steps=8):
    def block(t):
        return pl.BlockSpec((t.shape[0] // steps, t.shape[1]), lambda i: (i, 0))

    return pl.pallas_call(
        widen_kernel,
        grid=(steps,),
        out_shape=[jax.ShapeDtypeStruct(t.shape, F32) for t in arrays],
        in_specs=[block(t) for t in arrays],
        out_specs=[block(t) for t in arrays],
        compiler_params=pltpu.CompilerParams(vmem_limit_bytes=48 * 1024 * 1024),
        name="widen",
    )(*arrays)


def total_rows(m):
    return m.count * m.rows


def shards(
    image_big,
    image_small,
    view_big,
    view_small,
    inner_first,
    spatial_first,
    outer_first,
    norms_first,
    inner_second,
    spatial_second,
    outer_second,
    skip_second,
    norms_second,
    cotangent_big,
    cotangent_small,
):
    c3, c4 = inner_first.shape[1], inner_second.shape[1]
    weights = [
        inner_first,
        spatial_first.reshape(3, 3 * c3, c3),
        outer_first,
        inner_second,
        spatial_second.reshape(9 * c4, c4),
        outer_second,
        skip_second,
    ]
    sets, sizes, got = forward(
        [image_big, image_small], [cotangent_big, cotangent_small], (view_big, view_small), weights, norms_first, norms_second, 0
    )
    grad_b, grad_s, grads, sums = backward(
        sets, got, (view_big, view_small), weights, norms_first, norms_second, *sizes, (1, 2)
    )
    s1, s2, s3, s4, s5 = sums
    sq = got[21]

    def both(parts):
        return jnp.concatenate(
            [jnp.stack([t[g] + t[g + 1], t[0] + t[1]]) for t, g in parts], axis=1
        )

    g_skip, g_outer2, g_spatial2, g_inner2, g_outer1, g_spatial1, g_inner1 = widen(grads)
    results = [
        got[11][m.out0 : m.out0 + m.count * m.out].reshape(m.count, m.half, 8, -1)[:, :, : m.half]
        for m in sets
    ]
    gradients = [
        t.reshape(image.shape[0], image.shape[1], 16, -1)[:, :, : image.shape[2]]
        for t, image in ((grad_b, image_big), (grad_s, image_small))
    ]
    return (
        results[0],
        results[1],
        gradients[0],
        gradients[1],
        g_inner1,
        g_spatial1.reshape(spatial_first.shape),
        g_outer1,
        both(((s1, 2), (s2, 2), (s3, 2))),
        g_inner2,
        g_spatial2.reshape(spatial_second.shape),
        g_outer2,
        g_skip,
        both(((s4, 2), (s5, 2), (sq, 2), (sq, 4))),
    )


def solution(mesh):
    maps = P("crops", "rows", None, None)
    whole = P(("crops", "rows"), None, None, None)
    in_specs = (maps, maps, P("crops"), P("crops")) + (P(),) * 9 + (whole, whole)
    out_specs = (whole, whole, maps, maps) + (P(),) * 9
    return jax.shard_map(shards, mesh=mesh, in_specs=in_specs, out_specs=out_specs, check_vma=False)
```

profile of v0, /device:TPU:0, one launch (start us, length us, event | category | flops | bytes accessed | tf_op | source)
XLA Modules:
  0.0 327.3 jit_solution(18216409699214294924)
XLA Ops:
  0.6 0.0 copy-start.8
  0.7 1.3 copy.35
  2.0 0.2 pad.19.clone
  2.1 0.0 copy-done.8
  2.1 0.0 copy-start.7
  2.2 0.5 copy.34
  2.7 1.3 pad.17.clone
  4.0 0.0 copy-done.7
  4.0 0.4 pad.18
  4.3 0.0 copy-start.5
  4.3 1.5 pad_maximum_fusion.refs_6_
  5.8 1.0 copy-done.5
  6.8 2.1 pad.16
  8.9 113.3 %forward.1 = (bf16[1984,1024]{1,0:T(8,128)(2,1)}, f32[1984,256]{1,0:T(8,128)}, bf16[2160,768]{1,0:T(8,128)(2,1)}, f32[1984,256]{1,0:T(8,128)}, bf16[1984,256]{1,...) custom-call(s32[12]{0:T(128)} %refs_0_.5, ...), custom_call_target="tpu_custom_call" | custom-call | tf_op jit(solution)/shard_map/forward/pallas_call | solution.py:794
  122.2 1.1 slice_add_fusion.2
  123.3 1.1 slice.100
  124.5 2.6 slice.98
  127.0 1.1 copy.32
  128.1 68.4 %back_two.1 = (f32[1984,1024]{1,0:T(8,128)}, bf16[512,2048]{1,0:T(8,128)(2,1)}, bf16[1024,2048]{1,0:T(8,128)(2,1)}, bf16[4608,512]{1,0:T(8,128)(2,1)}, bf16[1024...) custom-call(s32[12]{0:T(128)} %refs_0_.5, s32[8]{0:T(128)} %refs_1_.5, ...), custom_call_target="tpu_custom_call" | custom-call | tf_op jit(solution)/shard_map/back_two/pallas_call | solution.py:1714
  196.5 0.0 copy-start.9
  196.5 0.0 copy-start.10
  196.5 0.0 copy-start.11
  196.5 106.5 %back_one.1 = (bf16[1344,1024]{1,0:T(8,128)(2,1)}, bf16[640,1024]{1,0:T(8,128)(2,1)}, f32[8,256]{1,0:T(8,128)}, f32[8,256]{1,0:T(8,128)}, bf16[1024,2048]{1,0:T(...) custom-call(s32[12]{0:T(128)} %refs_0_.5, ...), custom_call_target="tpu_custom_call" | custom-call | tf_op jit(solution)/shard_map/back_one/pallas_call | solution.py:1740
  303.0 0.0 copy-done.9
  303.0 0.0 copy-start
  303.1 2.8 copy.33
  305.9 0.9 slice_add_fusion.10
  306.7 0.6 maximum_maximum_fusion.1
  307.4 0.0 copy-done.10
  307.4 0.0 copy-done.11
  307.4 0.7 maximum_maximum_fusion
  308.0 0.0 copy-done
  308.0 0.0 copy-start.1
  308.0 1.3 copy-done.1
  309.3 0.0 copy-start.2
  309.3 1.2 copy-done.2
  310.5 0.0 copy-start.3
  310.5 1.0 copy-done.3
  311.6 0.0 copy-start.4
  311.6 1.0 copy-done.4
  312.6 0.0 copy-start.6
  312.6 13.0 %widen.1 = (f32[1024,2048]{1,0:T(8,128)}, f32[512,2048]{1,0:T(8,128)}, f32[4608,512]{1,0:T(8,128)}, f32[1024,512]{1,0:T(8,128)}, f32[256,1024]{1,0:T(8,128)}, /*index=5*/f32[2304,256]{1,0:T(8,128)}, f32[1024,256]{1,0:T(8,128)}) custom-call(bf16[1024,2048]{1,0:T(8,128)(2,1)} %get-tuple-element.88.refs_0_, bf16[512,2048]{1,0:T(8,128)(2,1)S(1)} %copy-done, ...), custom_call_target="tpu_custom_call" | custom-call | tf_op jit(solution)/shard_map/widen/pallas_call | solution.py:1761
  325.6 0.0 copy-done.6
  325.6 1.5 copy.37
  (2 shorter events, 0.0 us)
Async XLA Ops:
  0.6 1.5 copy-start.8
  2.1 1.8 copy-start.7
  4.3 2.5 copy-start.5
  196.5 106.5 %copy-start.9 = (f32[8,1024]{1,0:T(8,128)S(1)}, f32[8,1024]{1,0:T(8,128)}, u32[]{:S(2)}) copy-start(f32[8,1024]{1,0:T(8,128)} %get-tuple-element.77.refs_6_) | copy-start | bytes 98308
  196.5 110.8 %copy-start.10 = (f32[8,512]{1,0:T(8,128)S(1)}, f32[8,512]{1,0:T(8,128)}, u32[]{:S(2)}) copy-start(f32[8,512]{1,0:T(8,128)} %get-tuple-element.105) | copy-start | bytes 49156
  196.5 110.8 %copy-start.11 = (f32[8,512]{1,0:T(8,128)S(1)}, f32[8,512]{1,0:T(8,128)}, u32[]{:S(2)}) copy-start(f32[8,512]{1,0:T(8,128)} %get-tuple-element.104) | copy-start | bytes 49156
  303.0 5.0 %copy-start = (bf16[512,2048]{1,0:T(8,128)(2,1)S(1)}, bf16[512,2048]{1,0:T(8,128)(2,1)}, u32[]{:S(2)}) copy-start(bf16[512,2048]{1,0:T(8,128)(2,1)} %get-tuple-element.89.refs_1_) | copy-start | bytes 6291460
  308.0 1.3 copy-start.1
  309.3 1.2 copy-start.2
  310.5 1.0 copy-start.3
  311.6 1.0 copy-start.4
  312.6 13.0 %copy-start.6 = (bf16[1344,1024]{1,0:T(8,128)(2,1)S(1)}, bf16[1344,1024]{1,0:T(8,128)(2,1)}, u32[]{:S(2)}) copy-start(bf16[1344,1024]{1,0:T(8,128)(2,1)} %get-tuple-element.86) | copy-start | bytes 8257540
where the time goes:
time: 331 us; the launch traced here: 327 us
  Pallas kernels  301 us (91%)
  local copies, waits for them, and re-layouts  20.5 us (6%)
  other arithmetic  4.73 us (1%)
    pallas_call x1, Pallas kernels, forward(): pl.pallas_call(functools.partial(forward_kernel, sets, total, guarded, ou...  113 us
    pallas_call x1, Pallas kernels, backward(): pl.pallas_call(functools.partial(back_one_kernel, sets, total, guarded, c...  106 us
    pallas_call x1, Pallas kernels, backward(): pl.pallas_call(functools.partial(back_two_kernel, sets, total, outs, crop...  68.4 us
    pallas_call x1, Pallas kernels, widen(): pl.pallas_call(widen_kernel, grid=(steps,), out_shape=[jax.ShapeDtypeStru...  13 us
    unnamed x29, local copies, waits for them, and re-layouts  12.9 us

commit v1 on v0

--- a/solution.py
+++ b/solution.py
@@ -307,8 +307,8 @@
     c3, cin, c4, cout = dims
     (
         vb, vs, norms1, norms2,
-        img_b, img_s, cot_hbm, w1_h, wsp1_h, w3_h, w4_h, w5_h, w6_h, w7_h,
-    ), refs = refs[:14], refs[14:]
+        img_b, img_s, cot_b, cot_s, w1_h, wsp1_h, w3_h, w4_h, w5_h, w6_h, w7_h,
+    ), refs = refs[:15], refs[15:]
     (
         o_img, o_z1, o_h1, o_z2, o_h2, o_blk, o_z4, o_x5, o_z5, o_h5, o_xe, o_res, o_d6, o_d7,
         o_st1, o_st2, o_st3, o_st4, o_st7, o_st5, o_st6, o_sq, o_tally,
@@ -331,7 +331,8 @@
 
     loads = []
     for i, (src, dst) in enumerate(
-        ((w1_h, w1), (wsp1_h, wsp1), (w3_h, w3), (w4_h, w4), (w5_h, w5), (w6_h, w6), (w7_h, w7), (cot_hbm, cot))
+        ((w1_h, w1), (wsp1_h, wsp1), (w3_h, w3), (w4_h, w4), (w5_h, w5), (w6_h, w6), (w7_h, w7),
+            (cot_b, cot.at[0 : sets[1].out0]), (cot_s, cot.at[sets[1].out0 : outs]))
     ):
         loads.append(pltpu.make_async_copy(src, dst, load_sem.at[i]))
     own, swaps = [], []
@@ -645,6 +646,7 @@
     links.send_near(6, blocks[6])
     put(h5, o_h5)
     loads[7].wait()
+    loads[8].wait()
 
     def center(ms):
         for m in ms:
@@ -788,13 +790,13 @@
     scratch += [pltpu.SMEM((2, 16), F32), pltpu.VMEM((16, 128), F32)]
     scratch += exchange_shapes(FWD_WIDTHS, (3, 2, 2, 2, 2, 2, 2, 3), crops)
     scratch += [
-        pltpu.SemaphoreType.DMA((8,)), pltpu.SemaphoreType.DMA((nb + ns,)), pltpu.SemaphoreType.DMA((nb + ns,)),
+        pltpu.SemaphoreType.DMA((9,)), pltpu.SemaphoreType.DMA((nb + ns,)), pltpu.SemaphoreType.DMA((nb + ns,)),
         pltpu.SemaphoreType.DMA((nb + ns,)), pltpu.SemaphoreType.DMA((23,)),
     ]
     got = pl.pallas_call(
         functools.partial(forward_kernel, sets, total, guarded, outs, crops, (c3, cin, c4, cout)),
         out_shape=out_shape,
-        in_specs=[smem, smem, vmem, vmem] + [hbm] * 10,
+        in_specs=[smem, smem, vmem, vmem] + [hbm] * 11,
         out_specs=[hbm] * len(out_shape),
         scratch_shapes=scratch,
         compiler_params=pltpu.CompilerParams(
@@ -804,7 +806,7 @@
     )(
         *views, norms_first, norms_second,
         flat_rows(images[0], 16), flat_rows(images[1], 16),
-        jnp.concatenate([flat_rows(t, 8) for t in cots], axis=0), *w,
+        *[flat_rows(t, 8) for t in cots], *w,
     )
     return sets, (total, guarded, outs), got
 
@@ -1037,17 +1039,17 @@
 
 SHARE_CUTS = ((1, 2), (1, 1), (3, 1), (1, 1), (1, 1), (1, 1), (1, 1))
 SHARE_FIRST = 6
-SHARE_PATHS = (0, 1, 1, 0, 1, 0, 0, 0, 0, 0)
+SHARE_PATHS = (0, 1, 1, 0, 1, 0, 0, 0, 0, 1)
 SHARE_LATE = (
-    21, 51, 96, 83, 5, 37, -1, 97, -1, 22, 52, 6, -1, 98, -1, -1, -1, 53, -1, 23, 112, 84, 7, -1,
-    54, -1, 113, 8, 67, -1, -1, 55, 85, -1, 114, -1, 24, 99, 38, -1, 128, 86, 68, -1, 56, 115, 9, -1,
-    129, 69, -1, 116, 39, 100, -1, 10, -1, -1, 117, 144, 87, 25, 101, 118, 145, 57, 70, 130, 26, 88, 40, 102,
-    146, 58, 131, 119, 71, 147, 103, 120, 132, 148, 104, 133, 149, 89, 72, 121, 41, 150, 134, 122, 90, 151, 105, 42,
-    135, 73, 152, 106, 136, 74, 153, 154, 137, 138,
+    5, 51, 67, 96, 37, 21, -1, 97, -1, 6, -1, 52, 68, 98, 83, -1, -1, 7, 69, 38, -1, 99, -1, 112,
+    53, -1, 8, 113, 100, -1, 54, 84, -1, 114, 101, -1, -1, 55, 70, 85, -1, 9, 102, -1, 128, -1, 10, 56,
+    -1, 103, 115, 129, 39, 71, -1, -1, 116, -1, -1, 144, 104, 117, 145, 57, 118, 130, 86, 72, 58, 22, 146, 119,
+    105, 40, 131, 87, 106, 120, 147, 23, 132, 133, 148, 121, 73, 88, 149, 122, 134, 24, 41, 74, 150, 135, 42, 151,
+    89, 152, 136, 90, 25, 153, 26, 137, 154, 138,
 )
 SHARE_EARLY = (
-    32, -1, 33, 16, -1, -1, 17, 0, -1, 34, -1, 1, -1, 18, -1, 48, -1, -1, 35, -1, 64, 49, 2, -1,
-    65, 80, 19, -1, -1, 81, 3, 36, -1, -1, 66, 20, 37, 50, 4, -1, 82, -1, 21, 5, 51, 83, 67,
+    32, -1, 0, 33, 16, -1, 1, 17, -1, -1, -1, 34, -1, -1, 48, -1, 64, -1, -1, 80, 2, 18, 65, 35,
+    49, -1, -1, 81, 3, -1, 19, -1, -1, 4, 66, 50, 36, -1, 82, -1, 20, 5, 51, 37, 83, 67, 21,
 )
 
 

time: 331 us -> 340 us (1.027)
  Pallas kernels: 301 us -> 311 us
    pallas_call x1, Pallas kernels: 106 us -> 114 us  [backward(): pl.pallas_call(functools.partial(back_one_kernel, sets, total, guarded, c...]
where the time goes in v1:
time: 340 us; the launch traced here: 337 us
  Pallas kernels  311 us (91%)
  local copies, waits for them, and re-layouts  21.3 us (6%)
    pallas_call x1, Pallas kernels, backward(): pl.pallas_call(functools.partial(back_one_kernel, sets, total, guarded, c...  114 us
    pallas_call x1, Pallas kernels, forward(): pl.pallas_call(functools.partial(forward_kernel, sets, total, guarded, ou...  113 us
    pallas_call x1, Pallas kernels, backward(): pl.pallas_call(functools.partial(back_two_kernel, sets, total, outs, crop...  70.7 us
    pallas_call x1, Pallas kernels, widen(): pl.pallas_call(widen_kernel, grid=(steps,), out_shape=[jax.ShapeDtypeStru...  13 us
    unnamed x29, local copies, waits for them, and re-layouts  11.9 us

profile of v1, /device:TPU:0, one launch (start us, length us, event | category | flops | bytes accessed | tf_op | source)
XLA Modules:
  0.0 336.7 jit_solution(14812305093040598167)
XLA Ops:
  0.6 0.0 copy-start.8
  0.7 1.3 copy.35
  2.0 0.0 copy-start.7
  2.0 1.0 pad.19.clone
  3.0 0.0 copy-done.8
  3.0 0.5 copy.34
  3.5 0.0 copy-start.5
  3.5 1.3 pad.17.clone
  4.8 0.0 copy-done.7
  4.8 1.4 pad.18
  6.1 0.0 copy-done.5
  6.1 2.1 pad.16
  8.2 113.3 %forward.1 = (bf16[1984,1024]{1,0:T(8,128)(2,1)}, f32[1984,256]{1,0:T(8,128)}, bf16[2160,768]{1,0:T(8,128)(2,1)}, f32[1984,256]{1,0:T(8,128)}, bf16[1984,256]{1,...) custom-call(s32[12]{0:T(128)} %refs_0_.5, ...), custom_call_target="tpu_custom_call" | custom-call | tf_op jit(solution)/shard_map/forward/pallas_call | solution.py:796
  121.5 1.1 slice_add_fusion.2
  122.6 1.1 slice.100
  123.8 2.6 slice.98
  126.3 1.1 copy.32
  127.5 70.7 %back_two.1 = (f32[1984,1024]{1,0:T(8,128)}, bf16[512,2048]{1,0:T(8,128)(2,1)}, bf16[1024,2048]{1,0:T(8,128)(2,1)}, bf16[4608,512]{1,0:T(8,128)(2,1)}, bf16[1024...) custom-call(s32[12]{0:T(128)} %refs_0_.5, s32[8]{0:T(128)} %refs_1_.5, ...), custom_call_target="tpu_custom_call" | custom-call | tf_op jit(solution)/shard_map/back_two/pallas_call | solution.py:1716
  198.1 0.0 copy-start.9
  198.1 0.0 copy-start.10
  198.2 0.0 copy-start.11
  198.2 114.2 %back_one.1 = (bf16[1344,1024]{1,0:T(8,128)(2,1)}, bf16[640,1024]{1,0:T(8,128)(2,1)}, f32[8,256]{1,0:T(8,128)}, f32[8,256]{1,0:T(8,128)}, bf16[1024,2048]{1,0:T(...) custom-call(s32[12]{0:T(128)} %refs_0_.5, ...), custom_call_target="tpu_custom_call" | custom-call | tf_op jit(solution)/shard_map/back_one/pallas_call | solution.py:1742
  312.4 0.0 copy-done.9
  312.4 0.0 copy-start
  312.4 2.8 copy.33
  315.2 0.9 slice_add_fusion.10
  316.1 0.6 maximum_maximum_fusion.1
  316.7 0.0 copy-done.10
  316.7 0.0 copy-done.11
  316.7 0.7 maximum_maximum_fusion
  317.4 0.0 copy-done
  317.4 0.0 copy-start.1
  317.4 1.3 copy-done.1
  318.7 0.0 copy-start.2
  318.7 1.2 copy-done.2
  319.9 0.0 copy-start.3
  319.9 1.0 copy-done.3
  320.9 0.0 copy-start.4
  320.9 1.0 copy-done.4
  322.0 0.0 copy-start.6
  322.0 13.0 %widen.1 = (f32[1024,2048]{1,0:T(8,128)}, f32[512,2048]{1,0:T(8,128)}, f32[4608,512]{1,0:T(8,128)}, f32[1024,512]{1,0:T(8,128)}, f32[256,1024]{1,0:T(8,128)}, /*index=5*/f32[2304,256]{1,0:T(8,128)}, f32[1024,256]{1,0:T(8,128)}) custom-call(bf16[1024,2048]{1,0:T(8,128)(2,1)} %get-tuple-element.88.refs_0_, bf16[512,2048]{1,0:T(8,128)(2,1)S(1)} %copy-done, ...), custom_call_target="tpu_custom_call" | custom-call | tf_op jit(solution)/shard_map/widen/pallas_call | solution.py:1763
  335.0 0.0 copy-done.6
  335.0 1.5 copy.37
  (2 shorter events, 0.0 us)
Async XLA Ops:
  0.6 2.3 copy-start.8
  2.0 2.8 copy-start.7
  3.5 2.7 copy-start.5
  198.1 114.2 %copy-start.9 = (f32[8,1024]{1,0:T(8,128)S(1)}, f32[8,1024]{1,0:T(8,128)}, u32[]{:S(2)}) copy-start(f32[8,1024]{1,0:T(8,128)} %get-tuple-element.77.refs_6_) | copy-start | bytes 98308
  198.1 118.6 %copy-start.10 = (f32[8,512]{1,0:T(8,128)S(1)}, f32[8,512]{1,0:T(8,128)}, u32[]{:S(2)}) copy-start(f32[8,512]{1,0:T(8,128)} %get-tuple-element.105) | copy-start | bytes 49156
  198.2 118.6 %copy-start.11 = (f32[8,512]{1,0:T(8,128)S(1)}, f32[8,512]{1,0:T(8,128)}, u32[]{:S(2)}) copy-start(f32[8,512]{1,0:T(8,128)} %get-tuple-element.104) | copy-start | bytes 49156
  312.4 5.0 %copy-start = (bf16[512,2048]{1,0:T(8,128)(2,1)S(1)}, bf16[512,2048]{1,0:T(8,128)(2,1)}, u32[]{:S(2)}) copy-start(bf16[512,2048]{1,0:T(8,128)(2,1)} %get-tuple-element.89.refs_1_) | copy-start | bytes 6291460
  317.4 1.3 copy-start.1
  318.7 1.2 copy-start.2
  319.9 1.0 copy-start.3
  320.9 1.0 copy-start.4
  322.0 13.0 %copy-start.6 = (bf16[1344,1024]{1,0:T(8,128)(2,1)S(1)}, bf16[1344,1024]{1,0:T(8,128)(2,1)}, u32[]{:S(2)}) copy-start(bf16[1344,1024]{1,0:T(8,128)(2,1)} %get-tuple-element.86) | copy-start | bytes 8257540
